TPU v7x, 32 devices: a whole 2x2x4 slice. The times are simulated.
32 devices in a mesh: mirror: 2 (over y), rows: 4 (over z), cols: 4 (over x, core).
Axes of the slice: x: 2, y: 2, z: 4, core: 2. Of those that a mesh axis runs over, the one named last changes fastest.
Arguments:
- currents: bfloat16 [16, 131072], P(None, ('mirror', 'rows')), may hold values from -6 to 6
- right_side: float32 [16, 131072], P(None, ('mirror', 'rows', 'cols')), may hold values from -6 to 6
- geometry: float32 [4, 65536], replicated, may hold values from 0 to 4, as said below
Outputs:
- residual: float32 [16, 131072], P(None, ('mirror', 'rows', 'cols'))
- krylov_image: float32 [16, 131072], P(None, ('mirror', 'rows', 'cols'))
Inputs may be any that keep to these rules, and one draw needn't show every extreme that they name: `geometry`: rows are x in [0, 1], y in [0.05, 0.45], z in [0, 4] and a size in [0.003, 0.03].
All inputs are finite; a program needn't handle non-finite values.
Results may differ from a plain program's by a relative error of at most 0.0024.
Values may be sent and summed in bfloat16 or wider, within the bound.
No kernel may reach another device: no remote copies, remote signals or barrier semaphores. Data moves between devices by JAX's collectives and lax.ppermute only.
A program may use at most 64 MiB of HBM per device.

v0:
```python
import math

import jax
import jax.numpy as jnp
from jax import lax
from jax.sharding import PartitionSpec as P


def partner_2(block, axis, apart):
    count = lax.axis_size(axis)
    route = []
    for low in range(count):
        high = low | 1 << apart
        if high != low and high < count:
            route += [(low, high), (high, low)]
    return lax.ppermute(block, axis, route)


def kernel_block(row_geo, col_geo, reflect, scaling):
    diff_x = row_geo[0][:, None] - col_geo[0][None, :]
    diff_y = row_geo[1][:, None] - reflect * col_geo[1][None, :]
    diff_z = row_geo[2][:, None] - col_geo[2][None, :]
    spread = (row_geo[3] * row_geo[3])[:, None] + (col_geo[3] * col_geo[3])[None, :]
    squared = diff_x * diff_x + diff_y * diff_y + diff_z * diff_z + spread
    return (scaling / jnp.sqrt(squared)).astype(jnp.bfloat16)


def forward(stacked, source_geo, target_geo, reflect, scaling):
    excite = stacked.shape[1]
    target_len = target_geo.shape[1]
    block_len = min(1024, target_len)
    zero_sums = jnp.zeros((excite, 2, target_len), jnp.float32)

    def advance(position, totals):
        offset = position * block_len
        geo_part = lax.dynamic_slice_in_dim(target_geo, offset, block_len, 1)
        kernel_tile = kernel_block(source_geo, geo_part, reflect, scaling)
        partial_value = jnp.einsum(
            "hrs,st->rht", stacked, kernel_tile, preferred_element_type=jnp.float32
        )
        return lax.dynamic_update_slice_in_dim(totals, partial_value, offset, 2)

    totals = lax.fori_loop(0, target_len // block_len, advance, zero_sums)
    return totals.reshape(excite, 2 * target_len)


def on_device(currents, right_side, geometry):
    half_index = lax.axis_index("mirror")
    row_index = lax.axis_index("rows")
    col_index = lax.axis_index("cols")
    row_count = lax.axis_size("rows")
    col_count = lax.axis_size("cols")
    block_cells = currents.shape[1]
    piece_len = block_cells // col_count
    half_cells = geometry.shape[1]
    scaling = 1.0 / math.sqrt(2 * half_cells)
    reflect = 1.0 - 2.0 * half_index.astype(jnp.float32)
    block_geo = lax.dynamic_slice_in_dim(geometry, row_index * block_cells, block_cells, 1)
    strided_geo = lax.dynamic_index_in_dim(
        geometry.reshape(4, row_count, col_count, piece_len), col_index, 2, False
    ).reshape(4, row_count * piece_len)
    partner = partner_2(currents, "mirror", 0)
    partial_value = forward(
        jnp.stack([currents, partner]), block_geo, strided_geo, reflect, scaling
    )
    voltage = lax.psum_scatter(partial_value, ("mirror", "rows"), scatter_dimension=1, tiled=True)
    residual = right_side - voltage
    residual_b = residual.astype(jnp.bfloat16)
    block_cur = lax.all_gather(residual_b, "cols", axis=1, tiled=True)
    partner_block = partner_2(block_cur, "mirror", 0)
    partial_two = forward(
        jnp.stack([block_cur, partner_block]), block_geo, strided_geo, reflect, scaling
    )
    krylov_image = lax.psum_scatter(
        partial_two, ("mirror", "rows"), scatter_dimension=1, tiled=True
    )
    return (residual, krylov_image)


def solution(mesh):
    placed = (P(None, ("mirror", "rows")), P(None, ("mirror", "rows", "cols")), P())
    return jax.shard_map(
        on_device,
        mesh=mesh,
        in_specs=placed,
        out_specs=(P(None, ("mirror", "rows", "cols")), P(None, ("mirror", "rows", "cols"))),
        check_vma=False,
    )
```

profile of v0, /device:TPU:25, one launch (start us, length us, event | category | flops | bytes accessed | tf_op | source)
XLA Modules:
  0.0 1129.8 jit_solution(4809340316462908256)
XLA Ops:
  21.2 469.6 %while.28 = (s32[]{:T(128)}, f32[16,2,16384]{2,1,0:T(2,128)S(1)}, f32[4,16384]{1,0:T(4,128)S(1)}, f32[4,16384]{1,0:T(4,128)}, f32[]{:T(128)}, /*index=5*/f32[163...) while((s32[]{:T(128)}, f32[16,2,16384]{2,1,0:T(2,128)S(1)}, ...), condition=%wide.region_1.2_spmd, body=%wide.region_0.1_spmd.sunk | while | flops 1275070464 | bytes 2146543 | solution.py:43
  22.3 28.1 %fusion.34 = f32[16,2,1024]{2,0,1:T(8,128)S(1)} fusion(bf16[2,16,16384]{2,1,0:T(8,128)(2,1)S(1)} %get-tuple-element.472, f32[1024]{0:T(1024)S(1)} %bitcast.111, f32[16384]{0:T(1024)S(1)} %bitcast.116, f32[1024]{0:T(1024)S(1)} %bitcast.109, f32[16384]{0:T(1024)S(1)} %bitcast.98, f32[1024]{0:T(1024)S(1)} %bitcast.110, f32[16384]{0:T(1024)S(1)} %bitcast.99, ...), kind=kOutput, calls=%fused_computation.3.clone.2 | convolution fusion | flops 1275068416 | bytes 1458176 | tf_op jit(solution)/shard_map/while/body/eval_jaxpr/hrs,st->rht/dot_general | solution.py:38
  51.7 28.1 %fusion.34 = f32[16,2,1024]{2,0,1:T(8,128)S(1)} fusion(bf16[2,16,16384]{2,1,0:T(8,128)(2,1)S(1)} %get-tuple-element.472, f32[1024]{0:T(1024)S(1)} %bitcast.111, f32[16384]{0:T(1024)S(1)} %bitcast.116, f32[1024]{0:T(1024)S(1)} %bitcast.109, f32[16384]{0:T(1024)S(1)} %bitcast.98, f32[1024]{0:T(1024)S(1)} %bitcast.110, f32[16384]{0:T(1024)S(1)} %bitcast.99, ...), kind=kOutput, calls=%fused_computation.3.clone.2 | convolution fusion | flops 1275068416 | bytes 1458176 | tf_op jit(solution)/shard_map/while/body/eval_jaxpr/hrs,st->rht/dot_general | solution.py:38
  81.0 28.1 %fusion.34 = f32[16,2,1024]{2,0,1:T(8,128)S(1)} fusion(bf16[2,16,16384]{2,1,0:T(8,128)(2,1)S(1)} %get-tuple-element.472, f32[1024]{0:T(1024)S(1)} %bitcast.111, f32[16384]{0:T(1024)S(1)} %bitcast.116, f32[1024]{0:T(1024)S(1)} %bitcast.109, f32[16384]{0:T(1024)S(1)} %bitcast.98, f32[1024]{0:T(1024)S(1)} %bitcast.110, f32[16384]{0:T(1024)S(1)} %bitcast.99, ...), kind=kOutput, calls=%fused_computation.3.clone.2 | convolution fusion | flops 1275068416 | bytes 1458176 | tf_op jit(solution)/shard_map/while/body/eval_jaxpr/hrs,st->rht/dot_general | solution.py:38
  110.4 28.1 %fusion.34 = f32[16,2,1024]{2,0,1:T(8,128)S(1)} fusion(bf16[2,16,16384]{2,1,0:T(8,128)(2,1)S(1)} %get-tuple-element.472, f32[1024]{0:T(1024)S(1)} %bitcast.111, f32[16384]{0:T(1024)S(1)} %bitcast.116, f32[1024]{0:T(1024)S(1)} %bitcast.109, f32[16384]{0:T(1024)S(1)} %bitcast.98, f32[1024]{0:T(1024)S(1)} %bitcast.110, f32[16384]{0:T(1024)S(1)} %bitcast.99, ...), kind=kOutput, calls=%fused_computation.3.clone.2 | convolution fusion | flops 1275068416 | bytes 1458176 | tf_op jit(solution)/shard_map/while/body/eval_jaxpr/hrs,st->rht/dot_general | solution.py:38
  139.7 28.1 %fusion.34 = f32[16,2,1024]{2,0,1:T(8,128)S(1)} fusion(bf16[2,16,16384]{2,1,0:T(8,128)(2,1)S(1)} %get-tuple-element.472, f32[1024]{0:T(1024)S(1)} %bitcast.111, f32[16384]{0:T(1024)S(1)} %bitcast.116, f32[1024]{0:T(1024)S(1)} %bitcast.109, f32[16384]{0:T(1024)S(1)} %bitcast.98, f32[1024]{0:T(1024)S(1)} %bitcast.110, f32[16384]{0:T(1024)S(1)} %bitcast.99, ...), kind=kOutput, calls=%fused_computation.3.clone.2 | convolution fusion | flops 1275068416 | bytes 1458176 | tf_op jit(solution)/shard_map/while/body/eval_jaxpr/hrs,st->rht/dot_general | solution.py:38
  169.1 28.1 %fusion.34 = f32[16,2,1024]{2,0,1:T(8,128)S(1)} fusion(bf16[2,16,16384]{2,1,0:T(8,128)(2,1)S(1)} %get-tuple-element.472, f32[1024]{0:T(1024)S(1)} %bitcast.111, f32[16384]{0:T(1024)S(1)} %bitcast.116, f32[1024]{0:T(1024)S(1)} %bitcast.109, f32[16384]{0:T(1024)S(1)} %bitcast.98, f32[1024]{0:T(1024)S(1)} %bitcast.110, f32[16384]{0:T(1024)S(1)} %bitcast.99, ...), kind=kOutput, calls=%fused_computation.3.clone.2 | convolution fusion | flops 1275068416 | bytes 1458176 | tf_op jit(solution)/shard_map/while/body/eval_jaxpr/hrs,st->rht/dot_general | solution.py:38
  198.4 28.1 %fusion.34 = f32[16,2,1024]{2,0,1:T(8,128)S(1)} fusion(bf16[2,16,16384]{2,1,0:T(8,128)(2,1)S(1)} %get-tuple-element.472, f32[1024]{0:T(1024)S(1)} %bitcast.111, f32[16384]{0:T(1024)S(1)} %bitcast.116, f32[1024]{0:T(1024)S(1)} %bitcast.109, f32[16384]{0:T(1024)S(1)} %bitcast.98, f32[1024]{0:T(1024)S(1)} %bitcast.110, f32[16384]{0:T(1024)S(1)} %bitcast.99, ...), kind=kOutput, calls=%fused_computation.3.clone.2 | convolution fusion | flops 1275068416 | bytes 1458176 | tf_op jit(solution)/shard_map/while/body/eval_jaxpr/hrs,st->rht/dot_general | solution.py:38
  227.8 28.1 %fusion.34 = f32[16,2,1024]{2,0,1:T(8,128)S(1)} fusion(bf16[2,16,16384]{2,1,0:T(8,128)(2,1)S(1)} %get-tuple-element.472, f32[1024]{0:T(1024)S(1)} %bitcast.111, f32[16384]{0:T(1024)S(1)} %bitcast.116, f32[1024]{0:T(1024)S(1)} %bitcast.109, f32[16384]{0:T(1024)S(1)} %bitcast.98, f32[1024]{0:T(1024)S(1)} %bitcast.110, f32[16384]{0:T(1024)S(1)} %bitcast.99, ...), kind=kOutput, calls=%fused_computation.3.clone.2 | convolution fusion | flops 1275068416 | bytes 1458176 | tf_op jit(solution)/shard_map/while/body/eval_jaxpr/hrs,st->rht/dot_general | solution.py:38
  286.5 28.1 %fusion.34 = f32[16,2,1024]{2,0,1:T(8,128)S(1)} fusion(bf16[2,16,16384]{2,1,0:T(8,128)(2,1)S(1)} %get-tuple-element.472, f32[1024]{0:T(1024)S(1)} %bitcast.111, f32[16384]{0:T(1024)S(1)} %bitcast.116, f32[1024]{0:T(1024)S(1)} %bitcast.109, f32[16384]{0:T(1024)S(1)} %bitcast.98, f32[1024]{0:T(1024)S(1)} %bitcast.110, f32[16384]{0:T(1024)S(1)} %bitcast.99, ...), kind=kOutput, calls=%fused_computation.3.clone.2 | convolution fusion | flops 1275068416 | bytes 1458176 | tf_op jit(solution)/shard_map/while/body/eval_jaxpr/hrs,st->rht/dot_general | solution.py:38
  315.9 28.1 %fusion.34 = f32[16,2,1024]{2,0,1:T(8,128)S(1)} fusion(bf16[2,16,16384]{2,1,0:T(8,128)(2,1)S(1)} %get-tuple-element.472, f32[1024]{0:T(1024)S(1)} %bitcast.111, f32[16384]{0:T(1024)S(1)} %bitcast.116, f32[1024]{0:T(1024)S(1)} %bitcast.109, f32[16384]{0:T(1024)S(1)} %bitcast.98, f32[1024]{0:T(1024)S(1)} %bitcast.110, f32[16384]{0:T(1024)S(1)} %bitcast.99, ...), kind=kOutput, calls=%fused_computation.3.clone.2 | convolution fusion | flops 1275068416 | bytes 1458176 | tf_op jit(solution)/shard_map/while/body/eval_jaxpr/hrs,st->rht/dot_general | solution.py:38
  345.2 28.1 %fusion.34 = f32[16,2,1024]{2,0,1:T(8,128)S(1)} fusion(bf16[2,16,16384]{2,1,0:T(8,128)(2,1)S(1)} %get-tuple-element.472, f32[1024]{0:T(1024)S(1)} %bitcast.111, f32[16384]{0:T(1024)S(1)} %bitcast.116, f32[1024]{0:T(1024)S(1)} %bitcast.109, f32[16384]{0:T(1024)S(1)} %bitcast.98, f32[1024]{0:T(1024)S(1)} %bitcast.110, f32[16384]{0:T(1024)S(1)} %bitcast.99, ...), kind=kOutput, calls=%fused_computation.3.clone.2 | convolution fusion | flops 1275068416 | bytes 1458176 | tf_op jit(solution)/shard_map/while/body/eval_jaxpr/hrs,st->rht/dot_general | solution.py:38
  374.6 28.1 %fusion.34 = f32[16,2,1024]{2,0,1:T(8,128)S(1)} fusion(bf16[2,16,16384]{2,1,0:T(8,128)(2,1)S(1)} %get-tuple-element.472, f32[1024]{0:T(1024)S(1)} %bitcast.111, f32[16384]{0:T(1024)S(1)} %bitcast.116, f32[1024]{0:T(1024)S(1)} %bitcast.109, f32[16384]{0:T(1024)S(1)} %bitcast.98, f32[1024]{0:T(1024)S(1)} %bitcast.110, f32[16384]{0:T(1024)S(1)} %bitcast.99, ...), kind=kOutput, calls=%fused_computation.3.clone.2 | convolution fusion | flops 1275068416 | bytes 1458176 | tf_op jit(solution)/shard_map/while/body/eval_jaxpr/hrs,st->rht/dot_general | solution.py:38
  403.9 28.1 %fusion.34 = f32[16,2,1024]{2,0,1:T(8,128)S(1)} fusion(bf16[2,16,16384]{2,1,0:T(8,128)(2,1)S(1)} %get-tuple-element.472, f32[1024]{0:T(1024)S(1)} %bitcast.111, f32[16384]{0:T(1024)S(1)} %bitcast.116, f32[1024]{0:T(1024)S(1)} %bitcast.109, f32[16384]{0:T(1024)S(1)} %bitcast.98, f32[1024]{0:T(1024)S(1)} %bitcast.110, f32[16384]{0:T(1024)S(1)} %bitcast.99, ...), kind=kOutput, calls=%fused_computation.3.clone.2 | convolution fusion | flops 1275068416 | bytes 1458176 | tf_op jit(solution)/shard_map/while/body/eval_jaxpr/hrs,st->rht/dot_general | solution.py:38
  433.3 28.1 %fusion.34 = f32[16,2,1024]{2,0,1:T(8,128)S(1)} fusion(bf16[2,16,16384]{2,1,0:T(8,128)(2,1)S(1)} %get-tuple-element.472, f32[1024]{0:T(1024)S(1)} %bitcast.111, f32[16384]{0:T(1024)S(1)} %bitcast.116, f32[1024]{0:T(1024)S(1)} %bitcast.109, f32[16384]{0:T(1024)S(1)} %bitcast.98, f32[1024]{0:T(1024)S(1)} %bitcast.110, f32[16384]{0:T(1024)S(1)} %bitcast.99, ...), kind=kOutput, calls=%fused_computation.3.clone.2 | convolution fusion | flops 1275068416 | bytes 1458176 | tf_op jit(solution)/shard_map/while/body/eval_jaxpr/hrs,st->rht/dot_general | solution.py:38
  462.6 28.1 %fusion.34 = f32[16,2,1024]{2,0,1:T(8,128)S(1)} fusion(bf16[2,16,16384]{2,1,0:T(8,128)(2,1)S(1)} %get-tuple-element.472, f32[1024]{0:T(1024)S(1)} %bitcast.111, f32[16384]{0:T(1024)S(1)} %bitcast.116, f32[1024]{0:T(1024)S(1)} %bitcast.109, f32[16384]{0:T(1024)S(1)} %bitcast.98, f32[1024]{0:T(1024)S(1)} %bitcast.110, f32[16384]{0:T(1024)S(1)} %bitcast.99, ...), kind=kOutput, calls=%fused_computation.3.clone.2 | convolution fusion | flops 1275068416 | bytes 1458176 | tf_op jit(solution)/shard_map/while/body/eval_jaxpr/hrs,st->rht/dot_general | solution.py:38
  493.5 66.8 %reduce-scatter.3.cloned.1.call-done = f32[16,4096]{1,0:T(8,128)} async-done(((f32[16,32768]{1,0:T(8,128)}), f32[16,4096]{1,0:T(8,128)}) %reduce-scatter.3.cloned.1.call-update) | async-done | bytes 262160 | tf_op jit(solution)/shard_map/reduce_scatter | solution.py:66
  585.8 469.6 %while.29 = (s32[]{:T(128)}, f32[16,2,16384]{2,1,0:T(2,128)S(1)}, f32[4,16384]{1,0:T(4,128)S(1)}, f32[4,16384]{1,0:T(4,128)}, f32[]{:T(128)}, /*index=5*/f32[163...) while((s32[]{:T(128)}, f32[16,2,16384]{2,1,0:T(2,128)S(1)}, ...), condition=%wide.region_4.5_spmd, body=%wide.region_3.4_spmd.sunk | while | flops 1275070464 | bytes 2146543 | solution.py:43
  586.9 28.1 %fusion.38 = f32[16,2,1024]{2,0,1:T(8,128)S(1)} fusion(bf16[2,16,16384]{2,1,0:T(8,128)(2,1)S(1)} %get-tuple-element.514, f32[1024]{0:T(1024)S(1)} %bitcast.115, f32[16384]{0:T(1024)S(1)} %bitcast.117, f32[1024]{0:T(1024)S(1)} %bitcast.113, f32[16384]{0:T(1024)S(1)} %bitcast.101, f32[1024]{0:T(1024)S(1)} %bitcast.114, f32[16384]{0:T(1024)S(1)} %bitcast.102, ...), kind=kOutput, calls=%fused_computation.12.clone.1 | convolution fusion | flops 1275068416 | bytes 1458176 | tf_op jit(solution)/shard_map/while/body/eval_jaxpr/hrs,st->rht/dot_general | solution.py:38
  616.2 28.1 %fusion.38 = f32[16,2,1024]{2,0,1:T(8,128)S(1)} fusion(bf16[2,16,16384]{2,1,0:T(8,128)(2,1)S(1)} %get-tuple-element.514, f32[1024]{0:T(1024)S(1)} %bitcast.115, f32[16384]{0:T(1024)S(1)} %bitcast.117, f32[1024]{0:T(1024)S(1)} %bitcast.113, f32[16384]{0:T(1024)S(1)} %bitcast.101, f32[1024]{0:T(1024)S(1)} %bitcast.114, f32[16384]{0:T(1024)S(1)} %bitcast.102, ...), kind=kOutput, calls=%fused_computation.12.clone.1 | convolution fusion | flops 1275068416 | bytes 1458176 | tf_op jit(solution)/shard_map/while/body/eval_jaxpr/hrs,st->rht/dot_general | solution.py:38
  645.6 28.1 %fusion.38 = f32[16,2,1024]{2,0,1:T(8,128)S(1)} fusion(bf16[2,16,16384]{2,1,0:T(8,128)(2,1)S(1)} %get-tuple-element.514, f32[1024]{0:T(1024)S(1)} %bitcast.115, f32[16384]{0:T(1024)S(1)} %bitcast.117, f32[1024]{0:T(1024)S(1)} %bitcast.113, f32[16384]{0:T(1024)S(1)} %bitcast.101, f32[1024]{0:T(1024)S(1)} %bitcast.114, f32[16384]{0:T(1024)S(1)} %bitcast.102, ...), kind=kOutput, calls=%fused_computation.12.clone.1 | convolution fusion | flops 1275068416 | bytes 1458176 | tf_op jit(solution)/shard_map/while/body/eval_jaxpr/hrs,st->rht/dot_general | solution.py:38
  675.0 28.1 %fusion.38 = f32[16,2,1024]{2,0,1:T(8,128)S(1)} fusion(bf16[2,16,16384]{2,1,0:T(8,128)(2,1)S(1)} %get-tuple-element.514, f32[1024]{0:T(1024)S(1)} %bitcast.115, f32[16384]{0:T(1024)S(1)} %bitcast.117, f32[1024]{0:T(1024)S(1)} %bitcast.113, f32[16384]{0:T(1024)S(1)} %bitcast.101, f32[1024]{0:T(1024)S(1)} %bitcast.114, f32[16384]{0:T(1024)S(1)} %bitcast.102, ...), kind=kOutput, calls=%fused_computation.12.clone.1 | convolution fusion | flops 1275068416 | bytes 1458176 | tf_op jit(solution)/shard_map/while/body/eval_jaxpr/hrs,st->rht/dot_general | solution.py:38
  704.3 28.1 %fusion.38 = f32[16,2,1024]{2,0,1:T(8,128)S(1)} fusion(bf16[2,16,16384]{2,1,0:T(8,128)(2,1)S(1)} %get-tuple-element.514, f32[1024]{0:T(1024)S(1)} %bitcast.115, f32[16384]{0:T(1024)S(1)} %bitcast.117, f32[1024]{0:T(1024)S(1)} %bitcast.113, f32[16384]{0:T(1024)S(1)} %bitcast.101, f32[1024]{0:T(1024)S(1)} %bitcast.114, f32[16384]{0:T(1024)S(1)} %bitcast.102, ...), kind=kOutput, calls=%fused_computation.12.clone.1 | convolution fusion | flops 1275068416 | bytes 1458176 | tf_op jit(solution)/shard_map/while/body/eval_jaxpr/hrs,st->rht/dot_general | solution.py:38
  733.7 28.1 %fusion.38 = f32[16,2,1024]{2,0,1:T(8,128)S(1)} fusion(bf16[2,16,16384]{2,1,0:T(8,128)(2,1)S(1)} %get-tuple-element.514, f32[1024]{0:T(1024)S(1)} %bitcast.115, f32[16384]{0:T(1024)S(1)} %bitcast.117, f32[1024]{0:T(1024)S(1)} %bitcast.113, f32[16384]{0:T(1024)S(1)} %bitcast.101, f32[1024]{0:T(1024)S(1)} %bitcast.114, f32[16384]{0:T(1024)S(1)} %bitcast.102, ...), kind=kOutput, calls=%fused_computation.12.clone.1 | convolution fusion | flops 1275068416 | bytes 1458176 | tf_op jit(solution)/shard_map/while/body/eval_jaxpr/hrs,st->rht/dot_general | solution.py:38
  763.0 28.1 %fusion.38 = f32[16,2,1024]{2,0,1:T(8,128)S(1)} fusion(bf16[2,16,16384]{2,1,0:T(8,128)(2,1)S(1)} %get-tuple-element.514, f32[1024]{0:T(1024)S(1)} %bitcast.115, f32[16384]{0:T(1024)S(1)} %bitcast.117, f32[1024]{0:T(1024)S(1)} %bitcast.113, f32[16384]{0:T(1024)S(1)} %bitcast.101, f32[1024]{0:T(1024)S(1)} %bitcast.114, f32[16384]{0:T(1024)S(1)} %bitcast.102, ...), kind=kOutput, calls=%fused_computation.12.clone.1 | convolution fusion | flops 1275068416 | bytes 1458176 | tf_op jit(solution)/shard_map/while/body/eval_jaxpr/hrs,st->rht/dot_general | solution.py:38
  821.7 28.1 %fusion.38 = f32[16,2,1024]{2,0,1:T(8,128)S(1)} fusion(bf16[2,16,16384]{2,1,0:T(8,128)(2,1)S(1)} %get-tuple-element.514, f32[1024]{0:T(1024)S(1)} %bitcast.115, f32[16384]{0:T(1024)S(1)} %bitcast.117, f32[1024]{0:T(1024)S(1)} %bitcast.113, f32[16384]{0:T(1024)S(1)} %bitcast.101, f32[1024]{0:T(1024)S(1)} %bitcast.114, f32[16384]{0:T(1024)S(1)} %bitcast.102, ...), kind=kOutput, calls=%fused_computation.12.clone.1 | convolution fusion | flops 1275068416 | bytes 1458176 | tf_op jit(solution)/shard_map/while/body/eval_jaxpr/hrs,st->rht/dot_general | solution.py:38
  851.1 28.1 %fusion.38 = f32[16,2,1024]{2,0,1:T(8,128)S(1)} fusion(bf16[2,16,16384]{2,1,0:T(8,128)(2,1)S(1)} %get-tuple-element.514, f32[1024]{0:T(1024)S(1)} %bitcast.115, f32[16384]{0:T(1024)S(1)} %bitcast.117, f32[1024]{0:T(1024)S(1)} %bitcast.113, f32[16384]{0:T(1024)S(1)} %bitcast.101, f32[1024]{0:T(1024)S(1)} %bitcast.114, f32[16384]{0:T(1024)S(1)} %bitcast.102, ...), kind=kOutput, calls=%fused_computation.12.clone.1 | convolution fusion | flops 1275068416 | bytes 1458176 | tf_op jit(solution)/shard_map/while/body/eval_jaxpr/hrs,st->rht/dot_general | solution.py:38
  880.4 28.1 %fusion.38 = f32[16,2,1024]{2,0,1:T(8,128)S(1)} fusion(bf16[2,16,16384]{2,1,0:T(8,128)(2,1)S(1)} %get-tuple-element.514, f32[1024]{0:T(1024)S(1)} %bitcast.115, f32[16384]{0:T(1024)S(1)} %bitcast.117, f32[1024]{0:T(1024)S(1)} %bitcast.113, f32[16384]{0:T(1024)S(1)} %bitcast.101, f32[1024]{0:T(1024)S(1)} %bitcast.114, f32[16384]{0:T(1024)S(1)} %bitcast.102, ...), kind=kOutput, calls=%fused_computation.12.clone.1 | convolution fusion | flops 1275068416 | bytes 1458176 | tf_op jit(solution)/shard_map/while/body/eval_jaxpr/hrs,st->rht/dot_general | solution.py:38
  909.8 28.1 %fusion.38 = f32[16,2,1024]{2,0,1:T(8,128)S(1)} fusion(bf16[2,16,16384]{2,1,0:T(8,128)(2,1)S(1)} %get-tuple-element.514, f32[1024]{0:T(1024)S(1)} %bitcast.115, f32[16384]{0:T(1024)S(1)} %bitcast.117, f32[1024]{0:T(1024)S(1)} %bitcast.113, f32[16384]{0:T(1024)S(1)} %bitcast.101, f32[1024]{0:T(1024)S(1)} %bitcast.114, f32[16384]{0:T(1024)S(1)} %bitcast.102, ...), kind=kOutput, calls=%fused_computation.12.clone.1 | convolution fusion | flops 1275068416 | bytes 1458176 | tf_op jit(solution)/shard_map/while/body/eval_jaxpr/hrs,st->rht/dot_general | solution.py:38
  939.1 28.1 %fusion.38 = f32[16,2,1024]{2,0,1:T(8,128)S(1)} fusion(bf16[2,16,16384]{2,1,0:T(8,128)(2,1)S(1)} %get-tuple-element.514, f32[1024]{0:T(1024)S(1)} %bitcast.115, f32[16384]{0:T(1024)S(1)} %bitcast.117, f32[1024]{0:T(1024)S(1)} %bitcast.113, f32[16384]{0:T(1024)S(1)} %bitcast.101, f32[1024]{0:T(1024)S(1)} %bitcast.114, f32[16384]{0:T(1024)S(1)} %bitcast.102, ...), kind=kOutput, calls=%fused_computation.12.clone.1 | convolution fusion | flops 1275068416 | bytes 1458176 | tf_op jit(solution)/shard_map/while/body/eval_jaxpr/hrs,st->rht/dot_general | solution.py:38
  997.8 28.1 %fusion.38 = f32[16,2,1024]{2,0,1:T(8,128)S(1)} fusion(bf16[2,16,16384]{2,1,0:T(8,128)(2,1)S(1)} %get-tuple-element.514, f32[1024]{0:T(1024)S(1)} %bitcast.115, f32[16384]{0:T(1024)S(1)} %bitcast.117, f32[1024]{0:T(1024)S(1)} %bitcast.113, f32[16384]{0:T(1024)S(1)} %bitcast.101, f32[1024]{0:T(1024)S(1)} %bitcast.114, f32[16384]{0:T(1024)S(1)} %bitcast.102, ...), kind=kOutput, calls=%fused_computation.12.clone.1 | convolution fusion | flops 1275068416 | bytes 1458176 | tf_op jit(solution)/shard_map/while/body/eval_jaxpr/hrs,st->rht/dot_general | solution.py:38
  1058.0 65.0 %reduce-scatter.5.cloned.1.call-done = f32[16,4096]{1,0:T(8,128)} async-done(((f32[16,32768]{1,0:T(8,128)}), f32[16,4096]{1,0:T(8,128)}) %reduce-scatter.5.cloned.1.call-update) | async-done | bytes 262160 | tf_op jit(solution)/shard_map/reduce_scatter | solution.py:74
  (125 shorter events, 196.1 us)
Async XLA Ops:
  7.2 13.1 %copy-start = (bf16[16,16384]{1,0:T(8,128)(2,1)S(1)}, bf16[16,16384]{1,0:T(8,128)(2,1)}, u32[]{:S(2)}) copy-start(bf16[16,16384]{1,0:T(8,128)(2,1)} %param.7) | copy-start | bytes 1572868
  7.2 553.1 %reduce-scatter.3.cloned.1.call-start = ((), (), s32[]{:S(2)}) async-start(), calls=%async_computation.2 | async-start | bytes 2359296 | tf_op jit(solution)/shard_map/reduce_scatter | solution.py:66
  7.2 13.1 %collective-permute-start = (bf16[16,16384]{1,0:T(8,128)(2,1)}, bf16[16,16384]{1,0:T(8,128)(2,1)S(1)}, u32[]{:S(2)}, u32[]{:S(2)}) collective-permute-start(bf16[16,16384]{1,0:T(8,128)(2,1)} %param.7), channel_id=1, source_target_pairs={{0,16},{16,0},{1,17},{17,1},{2,18},{18,2},{3,19},{19,3},{4,20},{20... | collective-permute-start | bytes 1572872 | tf_op jit(solution)/shard_map/ppermute | solution.py:16
  493.4 66.9 %copy-start.1 = (f32[16,4096]{1,0:T(8,128)S(1)}, f32[16,4096]{1,0:T(8,128)}, u32[]{:S(2)}) copy-start(f32[16,4096]{1,0:T(8,128)} %param.8) | copy-start | bytes 786436
  493.4 629.5 %reduce-scatter.5.cloned.1.call-start = ((), (), s32[]{:S(2)}) async-start(), calls=%async_computation.3 | async-start | bytes 2359296 | tf_op jit(solution)/shard_map/reduce_scatter | solution.py:74
  571.5 13.4 %collective-permute-start.1 = (bf16[16,16384]{1,0:T(8,128)(2,1)S(1)}, bf16[16,16384]{1,0:T(8,128)(2,1)S(1)}, u32[]{:S(2)}, u32[]{:S(2)}) collective-permute-start(bf16[16,16384]{1,0:T(8,128)(2,1)S(1)} %all_gather.3), channel_id=1, source_target_pairs={{0,16},{16,0},{1,17},{17,1},{2,18},{18,2},{3,19},{19,3},{4,20},{20... | collective-permute-start | bytes 1572872 | tf_op jit(solution)/shard_map/ppermute | solution.py:16
Sparse Core Ops, SparseCore 0:
  493.5 66.6 reduce-scatter.2
  1058.1 64.8 reduce-scatter.4
where the time goes:
time: 1140 us; the launch traced here: 1130 us
  matrix products  899 us (79%)
  waiting for transfers between devices  151 us (13%)
  other arithmetic  34 us (3%)
  local copies, waits for them, and re-layouts  19.6 us (2%)
  between operations  14.1 us (1%)
    dot_general x32, matrix products, advance(): jnp.einsum('hrs,st->rht', stacked, kernel_tile, preferred_element_type=jn...  899 us
    reduce_scatter x1, waiting for transfers between devices, on_device(): lax.psum_scatter(partial_value, ('mirror', 'rows'), scatter_dimension=1,...  66.8 us
    reduce_scatter x1, waiting for transfers between devices, on_device(): lax.psum_scatter(partial_two, ('mirror', 'rows'), scatter_dimension=1, ti...  65 us
    slice x32, other arithmetic, kernel_block(): diff_x = row_geo[0][:, None] - col_geo[0][None, :]  30.9 us
  transfers between devices with their start and end apart: 4, of which 4 were waited for; matrix products, arithmetic and copies ran while one was open for 1% of the time, Pallas kernels for 0%

commit v1 on v0

v1 whole, which is shorter than its diff:
```python
import functools
import math

import jax
import jax.numpy as jnp
import numpy as np
from jax import lax
from jax.experimental import pallas as pl
from jax.experimental.pallas import tpu as pltpu
from jax.sharding import PartitionSpec as P

AXES = ("mirror", "rows", "cols")
F32 = jnp.float32
BF16 = jnp.bfloat16
SUB = 256
STRIP = 16
LAST = (((1,), (1,)), ((), ()))


class Plan:
    def __init__(self, pieces, half):
        self.pieces = pieces
        self.blocks = math.isqrt(4 * pieces)
        assert self.blocks * self.blocks == 4 * pieces and self.blocks % 4 == 0
        self.homes = self.blocks // 2
        self.per_half = pieces // self.blocks
        self.block_len = half // self.blocks
        self.piece_len = half // pieces
        self.tile = min(1024, self.block_len)
        self.tiles = self.block_len // self.tile

    def device(self, block, home):
        return home // self.per_half * self.pieces + block * self.per_half + home % self.per_half

    def route(self, near, step):
        pairs = []
        for block in range(self.blocks):
            for home in range(self.homes):
                other = block if near else (block + home + 1) % self.blocks
                source = self.device(other, (home + step) % self.homes)
                pairs.append((source, self.device(block, home)))
        return pairs

    def jobs(self):
        count = self.tiles
        pair = [(i, count + j) for i in range(count) for j in range(count)]
        diagonal = [
            (low + i, low + j) for low in (0, count) for i in range(count) for j in range(i + 1, count)
        ]
        tables = []
        for work in (pair, diagonal):
            table = np.zeros((3, count * count + 1), np.int32)
            for at, (i, j) in enumerate(work):
                table[:, at] = i, j, at == 0 or work[at - 1][0] != i
            tables.append(table)
        return tables[0], tables[1], len(pair), len(diagonal)


def operator_kernel(plan, table, counts, geo, *refs):
    pieces = refs[: plan.blocks]
    results = refs[plan.blocks : 2 * plan.blocks]
    drive, by_column, by_row, near, far, turned = refs[2 * plan.blocks :]
    tile, homes, piece_len = plan.tile, plan.homes, plan.piece_len
    chunks = tile // SUB
    strips = SUB // STRIP

    def place(index):
        home = lax.rem(counts[2] + index % homes, homes)
        half = home // plan.per_half
        offset = (index // homes) * plan.block_len + lax.rem(home, plan.per_half) * piece_len
        return half, pl.multiple_of(offset, 128)

    for index in range(plan.blocks):
        half, offset = place(index)
        value = pieces[index][...]
        drive[pl.ds(pl.multiple_of(half * 16, 16), 16), pl.ds(offset, piece_len)] = value
        drive[pl.ds(pl.multiple_of(48 - half * 16, 16), 16), pl.ds(offset, piece_len)] = value
    by_column[...] = jnp.zeros_like(by_column)
    by_row[...] = jnp.zeros_like(by_row)

    def turn(row0):
        for part in range(tile // 128):
            turned[part * 128 : part * 128 + 128, :] = jnp.transpose(geo[:, pl.ds(row0 + part * 128, 128)])

    def make(slot, row, col0, first, at, lanes=0):
        part = turned[row : row + STRIP, :]
        x_r, y_r, z_r, q_r = [jnp.broadcast_to(part[:, n : n + 1], (STRIP, 128)) for n in range(4)]
        for lane in range(lanes, tile, 128):
            cols = geo[:, pl.ds(col0 + lane, 128)]
            diff_x = x_r - cols[0:1]
            diff_z = z_r - cols[2:3]
            base = (q_r + cols[3:4]) + diff_x * diff_x + diff_z * diff_z
            cross = y_r * cols[4:5]
            near[slot, at : at + STRIP, lane : lane + 128] = lax.rsqrt(base - cross).astype(BF16)
            far[slot, at : at + STRIP, lane : lane + 128] = lax.rsqrt(base + cross).astype(BF16)

    def to_columns(slot, row0, col0, chunk):
        lanes = slice(chunk * SUB, chunk * SUB + SUB)
        rows = pl.ds(row0, SUB)
        by_column[:, pl.ds(col0 + chunk * SUB, SUB)] += jnp.dot(
            drive[0:32, rows], near[slot, :, lanes], preferred_element_type=F32
        ) + jnp.dot(drive[32:64, rows], far[slot, :, lanes], preferred_element_type=F32)

    def to_rows(slot, col0, chunk):
        lanes = slice(chunk * SUB, chunk * SUB + SUB)
        cols = pl.ds(col0 + chunk * SUB, SUB)
        return lax.dot_general(
            drive[0:32, cols], near[slot, :, lanes], LAST, preferred_element_type=F32
        ) + lax.dot_general(drive[32:64, cols], far[slot, :, lanes], LAST, preferred_element_type=F32)

    def pair_tile(at, carry):
        row0 = pl.multiple_of(table[0, at] * tile, tile)
        col0 = pl.multiple_of(table[1, at] * tile, tile)
        next0 = pl.multiple_of(table[1, at + 1] * tile, tile)

        @pl.when(table[2, at] == 1)
        def _():
            turn(row0)
            for strip in range(strips):
                make(0, strip * STRIP, col0, True, strip * STRIP)

        for sub in range(chunks):
            ahead, ahead0 = (sub + 1, col0) if sub + 1 < chunks else (0, next0)
            total = None
            for chunk in range(chunks):
                for strip in range(chunk * strips // chunks, (chunk + 1) * strips // chunks):
                    make((sub + 1) % 2, ahead * SUB + strip * STRIP, ahead0, False, strip * STRIP)
                to_columns(sub % 2, row0 + sub * SUB, col0, chunk)
                term = to_rows(sub % 2, col0, chunk)
                total = term if total is None else total + term
            by_row[:, pl.ds(row0 + sub * SUB, SUB)] += total
        return carry

    def diagonal_tile(at, carry):
        row0 = pl.multiple_of(at * tile, tile)
        turn(row0)
        for sub in range(chunks):
            slot = sub % 2
            for strip in range(strips):
                make(slot, sub * SUB + strip * STRIP, row0, False, strip * STRIP, sub * SUB)
            total = None
            for chunk in range(sub, chunks):
                to_columns(slot, row0 + sub * SUB, row0, chunk)
                if chunk > sub:
                    term = to_rows(slot, row0, chunk)
                    total = term if total is None else total + term
            if total is not None:
                by_row[:, pl.ds(row0 + sub * SUB, SUB)] += total
        return carry

    lax.fori_loop(0, counts[0], pair_tile, 0)
    lax.fori_loop(0, counts[1], diagonal_tile, 0)

    for index in range(plan.blocks):
        half, offset = place(index)
        rows = pl.ds(pl.multiple_of(half * 16, 16), 16)
        cols = pl.ds(offset, piece_len)
        results[index][...] = by_column[rows, cols] + by_row[rows, cols]


def apply_operator(plan, table, counts, geo, pieces):
    cells = 2 * plan.block_len
    vmem = pl.BlockSpec(memory_space=pltpu.VMEM)
    smem = pl.BlockSpec(memory_space=pltpu.SMEM)
    return pl.pallas_call(
        functools.partial(operator_kernel, plan),
        in_specs=[smem, smem, vmem] + [vmem] * plan.blocks,
        out_specs=[vmem] * plan.blocks,
        out_shape=[jax.ShapeDtypeStruct((16, plan.piece_len), F32)] * plan.blocks,
        scratch_shapes=[
            pltpu.VMEM((64, cells), BF16),
            pltpu.VMEM((32, cells), F32),
            pltpu.VMEM((32, cells), F32),
            pltpu.VMEM((2, SUB, plan.tile), BF16),
            pltpu.VMEM((2, SUB, plan.tile), BF16),
            pltpu.VMEM((plan.tile, 8), F32),
        ],
        compiler_params=pltpu.CompilerParams(vmem_limit_bytes=40 * 2**20),
        name="peec_pairs",
    )(table, counts, geo, *pieces)


def gather_pieces(plan, own):
    pieces = [own]
    for step in range(1, plan.homes):
        pieces.append(lax.ppermute(own, AXES, plan.route(True, step)))
    for step in range(plan.homes):
        pieces.append(lax.ppermute(own, AXES, plan.route(False, step)))
    return pieces


def return_pieces(plan, partials):
    total = partials[0]
    for index in range(1, plan.blocks):
        route = plan.route(index < plan.homes, index % plan.homes)
        back = [(target, source) for source, target in route]
        total = total + lax.ppermute(partials[index], AXES, back)
    return total


def local_geometry(plan, geometry, block, partner):
    scale = math.sqrt(2 * geometry.shape[1])
    length = plan.block_len
    cells = jnp.concatenate(
        [lax.dynamic_slice_in_dim(geometry, at * length, length, 1) for at in (block, partner)], axis=1
    )
    x, y, z, size = [cells[n] * scale for n in range(4)]
    zero = jnp.zeros_like(x)
    return jnp.stack([x, y, z, y * y + size * size, y + y, zero, zero, zero])


def on_device(plan, currents, right_side, geometry):
    piece = lax.axis_index("rows") * lax.axis_size("cols") + lax.axis_index("cols")
    block = piece // plan.per_half
    home = lax.axis_index("mirror") * plan.per_half + piece % plan.per_half
    partner = (block + home + 1) % plan.blocks
    pair, diagonal, pair_count, diagonal_count = plan.jobs()
    on_diagonal = (home == plan.homes - 1) & (block >= plan.homes)
    table = jnp.where(on_diagonal, diagonal, pair)
    counts = jnp.stack(
        [
            jnp.where(on_diagonal, diagonal_count, pair_count),
            jnp.where(on_diagonal, 2 * plan.tiles, 0),
            home,
        ]
    ).astype(jnp.int32)
    geo = local_geometry(plan, geometry, block, partner)

    own = lax.dynamic_slice_in_dim(currents, lax.axis_index("cols") * plan.piece_len, plan.piece_len, 1)
    partials = apply_operator(plan, table, counts, geo, gather_pieces(plan, own))
    residual = right_side - return_pieces(plan, partials)
    partials = apply_operator(plan, table, counts, geo, gather_pieces(plan, residual.astype(BF16)))
    return residual, return_pieces(plan, partials)


def solution(mesh):
    pieces = mesh.shape["rows"] * mesh.shape["cols"]

    def whole(currents, right_side, geometry):
        plan = Plan(pieces, geometry.shape[1])
        return jax.shard_map(
            functools.partial(on_device, plan),
            mesh=mesh,
            in_specs=(P(None, ("mirror", "rows")), P(None, AXES), P()),
            out_specs=(P(None, AXES), P(None, AXES)),
            check_vma=False,
        )(currents, right_side, geometry)

    return whole
```

time: 1140 us -> 583 us (0.51)
  matrix products: 899 us -> 0 us
  Pallas kernels: 0 us -> 420 us
  starting transfers between devices: 1.67 us -> 64.1 us
  waiting for transfers between devices: 151 us -> 92.7 us
  other arithmetic: 34 us -> 2.17 us
  local copies, waits for them, and re-layouts: 19.6 us -> 2.86 us
  between operations: 14.1 us -> 0.85 us
    dot_general x32 -> x0, matrix products: 899 us -> none  [advance(): jnp.einsum('hrs,st->rht', stacked, kernel_tile, preferred_element_type=jn...]
    pallas_call x0 -> x2, Pallas kernels: none -> 420 us  [apply_operator(): pl.pallas_call(functools.partial(operator_kernel, plan), in_specs=[smem,...]
    reduce_scatter x2 -> x0, waiting for transfers between devices: 132 us -> none  [the longest x1 66.8 us: on_device(): lax.psum_scatter(partial_value, ('mirror', 'rows'), scatter_dimension=1,...]
    ppermute x2 -> x28, waiting for transfers between devices: 18.9 us -> 92.7 us  [the longest x14 80.1 us: return_pieces(): total = total + lax.ppermute(partials[index], AXES, back)]
    ppermute x2 -> x28, starting transfers between devices: 1.59 us -> 64.1 us  [the longest x14 43.2 us: return_pieces(): total = total + lax.ppermute(partials[index], AXES, back)]
    slice x32 -> x0, other arithmetic: 30.9 us -> none  [kernel_block(): diff_x = row_geo[0][:, None] - col_geo[0][None, :]]
  transfers between devices with their start and end apart: 4 -> 28, of which waited for: 4 -> 17; matrix products, arithmetic and copies ran while one was open for 1% -> 0% of each run, Pallas kernels for 0% -> 0%
where the time goes in v1:
time: 583 us
  Pallas kernels  420 us (72%)
  waiting for transfers between devices  92.7 us (16%)
  starting transfers between devices  64.1 us (11%)
    pallas_call x2, Pallas kernels, apply_operator(): pl.pallas_call(functools.partial(operator_kernel, plan), in_specs=[smem,...  420 us
    ppermute x14, waiting for transfers between devices, return_pieces(): total = total + lax.ppermute(partials[index], AXES, back)  80.1 us
    ppermute x14, starting transfers between devices, return_pieces(): total = total + lax.ppermute(partials[index], AXES, back)  43.2 us
    ppermute x6, starting transfers between devices, gather_pieces(): pieces.append(lax.ppermute(own, AXES, plan.route(True, step)))  14.8 us
  transfers between devices with their start and end apart: 28, of which 17 were waited for; matrix products, arithmetic and copies ran while one was open for 0% of the time, Pallas kernels for 0%

profile of v1, /device:TPU:25, one launch (start us, length us, event | category | flops | bytes accessed | tf_op | source)
XLA Modules:
  0.0 583.0 jit_solution(520868456353128201)
XLA Ops:
  0.6 1.0 copy-done
  1.7 2.6 collective-permute-start.6
  4.4 2.5 collective-permute-start.4
  6.8 0.9 collective-permute-start.3
  7.7 1.8 collective-permute-start.2
  9.5 1.0 constant_dynamic-slice_fusion.2
  10.9 9.4 %collective-permute-start.1 = (bf16[16,4096]{1,0:T(8,128)(2,1)S(1)}, bf16[16,4096]{1,0:T(8,128)(2,1)S(1)}, u32[]{:S(2)}, u32[]{:S(2)}) collective-permute-start(bf16[16,4096]{1,0:T(8,128)(2,1)S(1)} %constant_dynamic-slice_fusion.refs_0_), channel_id=1, source_target_pairs={{16,0},{17,1},{0,16},{1,17},{18,2},{19,3},{2,18},{3,19},{20,4},{21... | collective-permute-start | bytes 393224 | tf_op jit(solution)/shard_map/ppermute | solution.py:186
  20.4 0.7 stack.28.geo
  21.2 2.8 collective-permute-done.1.refs_2_
  24.7 210.1 %peec_pairs.2 = (f32[16,4096]{1,0:T(8,128)S(1)}, f32[16,4096]{1,0:T(8,128)S(1)}, f32[16,4096]{1,0:T(8,128)S(1)}, f32[16,4096]{1,0:T(8,128)S(1)}, f32[16,4096]{1,...) custom-call(s32[3,65]{1,0:T(4,128)S(1)} %broadcast_select_fusion.table, ...), custom_call_target="tpu_custom_call" | custom-call | tf_op jit(solution)/shard_map/peec_pairs/pallas_call | solution.py:165
  234.8 1.2 collective-permute-start.7
  236.0 16.5 %collective-permute-start.8 = (f32[16,4096]{1,0:T(8,128)S(1)}, f32[16,4096]{1,0:T(8,128)S(1)}, u32[]{:S(2)}, u32[]{:S(2)}) collective-permute-start(f32[16,4096]{1,0:T(8,128)S(1)} %get-tuple-element.20), channel_id=1, source_target_pairs={{0,16},{1,17},{16,0},{17,1},{2,18},{3,19},{18,2},{19,3},{4,20},{5,... | collective-permute-start | bytes 786440 | tf_op jit(solution)/shard_map/ppermute | solution.py:197
  253.3 11.0 %collective-permute-done.8 = f32[16,4096]{1,0:T(8,128)S(1)} collective-permute-done((f32[16,4096]{1,0:T(8,128)S(1)}, f32[16,4096]{1,0:T(8,128)S(1)}, u32[]{:S(2)}, u32[]{:S(2)}) %collective-permute-start.8) | collective-permute-done | bytes 262176 | tf_op jit(solution)/shard_map/ppermute | solution.py:197
  264.3 0.9 collective-permute-done.9
  265.1 3.4 collective-permute-done.11
  268.5 9.9 %collective-permute-done.12 = f32[16,4096]{1,0:T(8,128)S(1)} collective-permute-done((f32[16,4096]{1,0:T(8,128)S(1)}, f32[16,4096]{1,0:T(8,128)S(1)}, u32[]{:S(2)}, u32[]{:S(2)}) %collective-permute-start.12) | collective-permute-done | bytes 262176 | tf_op jit(solution)/shard_map/ppermute | solution.py:197
  278.5 14.9 %collective-permute-done.13 = f32[16,4096]{1,0:T(8,128)S(1)} collective-permute-done((f32[16,4096]{1,0:T(8,128)S(1)}, f32[16,4096]{1,0:T(8,128)S(1)}, u32[]{:S(2)}, u32[]{:S(2)}) %collective-permute-start.13) | collective-permute-done | bytes 262176 | tf_op jit(solution)/shard_map/ppermute | solution.py:197
  293.4 0.9 fusion.8
  294.3 3.7 collective-permute-start.16
  298.0 4.0 collective-permute-done.20.refs_7_
  302.0 1.6 collective-permute-done.18.refs_5_
  303.6 1.9 collective-permute-done.17.refs_4_
  305.5 1.1 collective-permute-done.15.refs_2_
  307.2 210.3 %peec_pairs.3 = (f32[16,4096]{1,0:T(8,128)S(1)}, f32[16,4096]{1,0:T(8,128)S(1)}, f32[16,4096]{1,0:T(8,128)S(1)}, f32[16,4096]{1,0:T(8,128)S(1)}, f32[16,4096]{1,...) custom-call(s32[3,65]{1,0:T(4,128)S(1)} %broadcast_select_fusion.table, ...), custom_call_target="tpu_custom_call" | custom-call | tf_op jit(solution)/shard_map/peec_pairs/pallas_call | solution.py:165
  517.5 7.5 %collective-permute-start.21 = (f32[16,4096]{1,0:T(8,128)S(1)}, f32[16,4096]{1,0:T(8,128)S(1)}, u32[]{:S(2)}, u32[]{:S(2)}) collective-permute-start(f32[16,4096]{1,0:T(8,128)S(1)} %get-tuple-element.27), channel_id=1, source_target_pairs={{0,1},{1,16},{16,17},{17,0},{2,3},{3,18},{18,19},{19,2},{4,5},{5,2... | collective-permute-start | bytes 786440 | tf_op jit(solution)/shard_map/ppermute | solution.py:197
  524.9 16.5 %collective-permute-start.22 = (f32[16,4096]{1,0:T(8,128)S(1)}, f32[16,4096]{1,0:T(8,128)S(1)}, u32[]{:S(2)}, u32[]{:S(2)}) collective-permute-start(f32[16,4096]{1,0:T(8,128)S(1)} %get-tuple-element.28), channel_id=1, source_target_pairs={{0,16},{1,17},{16,0},{17,1},{2,18},{3,19},{18,2},{19,3},{4,20},{5,... | collective-permute-start | bytes 786440 | tf_op jit(solution)/shard_map/ppermute | solution.py:197
  542.2 11.0 %collective-permute-done.22 = f32[16,4096]{1,0:T(8,128)S(1)} collective-permute-done((f32[16,4096]{1,0:T(8,128)S(1)}, f32[16,4096]{1,0:T(8,128)S(1)}, u32[]{:S(2)}, u32[]{:S(2)}) %collective-permute-start.22) | collective-permute-done | bytes 262176 | tf_op jit(solution)/shard_map/ppermute | solution.py:197
  553.2 0.9 collective-permute-done.23
  554.1 3.4 collective-permute-done.25
  557.5 10.0 %collective-permute-done.26 = f32[16,4096]{1,0:T(8,128)S(1)} collective-permute-done((f32[16,4096]{1,0:T(8,128)S(1)}, f32[16,4096]{1,0:T(8,128)S(1)}, u32[]{:S(2)}, u32[]{:S(2)}) %collective-permute-start.26) | collective-permute-done | bytes 262176 | tf_op jit(solution)/shard_map/ppermute | solution.py:197
  567.4 14.8 %collective-permute-done.27 = f32[16,4096]{1,0:T(8,128)S(1)} collective-permute-done((f32[16,4096]{1,0:T(8,128)S(1)}, f32[16,4096]{1,0:T(8,128)S(1)}, u32[]{:S(2)}, u32[]{:S(2)}) %collective-permute-start.27) | collective-permute-done | bytes 262176 | tf_op jit(solution)/shard_map/ppermute | solution.py:197
  582.2 0.8 add_add_fusion
  (45 shorter events, 3.5 us)
Async XLA Ops:
  0.6 1.0 copy-start
  1.7 9.2 %collective-permute-start.6 = (bf16[16,4096]{1,0:T(8,128)(2,1)S(1)}, bf16[16,4096]{1,0:T(8,128)(2,1)S(1)}, u32[]{:S(2)}, u32[]{:S(2)}) collective-permute-start(bf16[16,4096]{1,0:T(8,128)(2,1)S(1)} %constant_dynamic-slice_fusion.refs_0_), channel_id=1, source_target_pairs={{19,0},{4,1},{7,16},{24,17},{21,2},{6,3},{9,18},{26,19},{23,4},{8,... | collective-permute-start | bytes 393224 | tf_op jit(solution)/shard_map/ppermute | solution.py:188
  4.2 16.0 %collective-permute-start.5 = (bf16[16,4096]{1,0:T(8,128)(2,1)S(1)}, bf16[16,4096]{1,0:T(8,128)(2,1)S(1)}, u32[]{:S(2)}, u32[]{:S(2)}) collective-permute-start(bf16[16,4096]{1,0:T(8,128)(2,1)S(1)} %constant_dynamic-slice_fusion.refs_0_), channel_id=1, source_target_pairs={{18,0},{21,1},{6,16},{9,17},{20,2},{23,3},{8,18},{11,19},{22,4},{2... | collective-permute-start | bytes 393224 | tf_op jit(solution)/shard_map/ppermute | solution.py:188
  4.4 16.9 %collective-permute-start.4 = (bf16[16,4096]{1,0:T(8,128)(2,1)S(1)}, bf16[16,4096]{1,0:T(8,128)(2,1)S(1)}, u32[]{:S(2)}, u32[]{:S(2)}) collective-permute-start(bf16[16,4096]{1,0:T(8,128)(2,1)S(1)} %constant_dynamic-slice_fusion.refs_0_), channel_id=1, source_target_pairs={{3,0},{20,1},{23,16},{8,17},{5,2},{22,3},{25,18},{10,19},{7,4},{24... | collective-permute-start | bytes 393224 | tf_op jit(solution)/shard_map/ppermute | solution.py:188
  6.8 14.4 %collective-permute-start.3 = (bf16[16,4096]{1,0:T(8,128)(2,1)S(1)}, bf16[16,4096]{1,0:T(8,128)(2,1)S(1)}, u32[]{:S(2)}, u32[]{:S(2)}) collective-permute-start(bf16[16,4096]{1,0:T(8,128)(2,1)S(1)} %constant_dynamic-slice_fusion.refs_0_), channel_id=1, source_target_pairs={{2,0},{5,1},{22,16},{25,17},{4,2},{7,3},{24,18},{27,19},{6,4},{9,5... | collective-permute-start | bytes 393224 | tf_op jit(solution)/shard_map/ppermute | solution.py:188
  7.7 13.6 %collective-permute-start.2 = (bf16[16,4096]{1,0:T(8,128)(2,1)S(1)}, bf16[16,4096]{1,0:T(8,128)(2,1)S(1)}, u32[]{:S(2)}, u32[]{:S(2)}) collective-permute-start(bf16[16,4096]{1,0:T(8,128)(2,1)S(1)} %constant_dynamic-slice_fusion.refs_0_), channel_id=1, source_target_pairs={{17,0},{0,1},{1,16},{16,17},{19,2},{2,3},{3,18},{18,19},{21,4},{4,... | collective-permute-start | bytes 393224 | tf_op jit(solution)/shard_map/ppermute | solution.py:186
  10.9 9.4 %copy-start.3 = (s32[3,65]{1,0:T(4,128)S(1)}, s32[3,65]{1,0:T(4,128)}, u32[]{:S(2)}) copy-start(s32[3,65]{1,0:T(4,128)} %constant.76.clone) | copy-start | bytes 2344
  10.9 9.4 %copy-start.2 = (s32[3,65]{1,0:T(4,128)S(1)}, s32[3,65]{1,0:T(4,128)}, u32[]{:S(2)}) copy-start(s32[3,65]{1,0:T(4,128)} %constant.77.clone) | copy-start | bytes 2344
  10.9 13.2 %collective-permute-start.1 = (bf16[16,4096]{1,0:T(8,128)(2,1)S(1)}, bf16[16,4096]{1,0:T(8,128)(2,1)S(1)}, u32[]{:S(2)}, u32[]{:S(2)}) collective-permute-start(bf16[16,4096]{1,0:T(8,128)(2,1)S(1)} %constant_dynamic-slice_fusion.refs_0_), channel_id=1, source_target_pairs={{16,0},{17,1},{0,16},{1,17},{18,2},{19,3},{2,18},{3,19},{20,4},{21... | collective-permute-start | bytes 393224 | tf_op jit(solution)/shard_map/ppermute | solution.py:186
  20.3 4.4 collective-permute-start
  21.2 272.1 %copy-start.1 = (f32[16,4096]{1,0:T(8,128)S(1)}, f32[16,4096]{1,0:T(8,128)}, u32[]{:S(2)}) copy-start(f32[16,4096]{1,0:T(8,128)} %param.6) | copy-start | bytes 786436
  234.8 18.4 %collective-permute-start.7 = (f32[16,4096]{1,0:T(8,128)S(1)}, f32[16,4096]{1,0:T(8,128)S(1)}, u32[]{:S(2)}, u32[]{:S(2)}) collective-permute-start(f32[16,4096]{1,0:T(8,128)S(1)} %get-tuple-element.19), channel_id=1, source_target_pairs={{0,1},{1,16},{16,17},{17,0},{2,3},{3,18},{18,19},{19,2},{4,5},{5,2... | collective-permute-start | bytes 786440 | tf_op jit(solution)/shard_map/ppermute | solution.py:197
  236.0 28.3 %collective-permute-start.8 = (f32[16,4096]{1,0:T(8,128)S(1)}, f32[16,4096]{1,0:T(8,128)S(1)}, u32[]{:S(2)}, u32[]{:S(2)}) collective-permute-start(f32[16,4096]{1,0:T(8,128)S(1)} %get-tuple-element.20), channel_id=1, source_target_pairs={{0,16},{1,17},{16,0},{17,1},{2,18},{3,19},{18,2},{19,3},{4,20},{5,... | collective-permute-start | bytes 786440 | tf_op jit(solution)/shard_map/ppermute | solution.py:197
  252.5 12.7 %collective-permute-start.9 = (f32[16,4096]{1,0:T(8,128)S(1)}, f32[16,4096]{1,0:T(8,128)S(1)}, u32[]{:S(2)}, u32[]{:S(2)}) collective-permute-start(f32[16,4096]{1,0:T(8,128)S(1)} %get-tuple-element.21), channel_id=1, source_target_pairs={{0,17},{1,0},{16,1},{17,16},{2,19},{3,2},{18,3},{19,18},{4,21},{5,... | collective-permute-start | bytes 786440 | tf_op jit(solution)/shard_map/ppermute | solution.py:197
  253.2 11.9 %collective-permute-start.10 = (f32[16,4096]{1,0:T(8,128)S(1)}, f32[16,4096]{1,0:T(8,128)S(1)}, u32[]{:S(2)}, u32[]{:S(2)}) collective-permute-start(f32[16,4096]{1,0:T(8,128)S(1)} %get-tuple-element.22), channel_id=1, source_target_pairs={{0,2},{1,5},{16,22},{17,25},{2,4},{3,7},{18,24},{19,27},{4,6},{5,9... | collective-permute-start | bytes 786440 | tf_op jit(solution)/shard_map/ppermute | solution.py:197
  253.2 15.3 %collective-permute-start.11 = (f32[16,4096]{1,0:T(8,128)S(1)}, f32[16,4096]{1,0:T(8,128)S(1)}, u32[]{:S(2)}, u32[]{:S(2)}) collective-permute-start(f32[16,4096]{1,0:T(8,128)S(1)} %get-tuple-element.23), channel_id=1, source_target_pairs={{0,3},{1,20},{16,23},{17,8},{2,5},{3,22},{18,25},{19,10},{4,7},{5,... | collective-permute-start | bytes 786440 | tf_op jit(solution)/shard_map/ppermute | solution.py:197
  253.2 25.3 %collective-permute-start.12 = (f32[16,4096]{1,0:T(8,128)S(1)}, f32[16,4096]{1,0:T(8,128)S(1)}, u32[]{:S(2)}, u32[]{:S(2)}) collective-permute-start(f32[16,4096]{1,0:T(8,128)S(1)} %get-tuple-element.24), channel_id=1, source_target_pairs={{0,18},{1,21},{16,6},{17,9},{2,20},{3,23},{18,8},{19,11},{4,22},{5... | collective-permute-start | bytes 786440 | tf_op jit(solution)/shard_map/ppermute | solution.py:197
  264.3 29.1 %collective-permute-start.13 = (f32[16,4096]{1,0:T(8,128)S(1)}, f32[16,4096]{1,0:T(8,128)S(1)}, u32[]{:S(2)}, u32[]{:S(2)}) collective-permute-start(f32[16,4096]{1,0:T(8,128)S(1)} %get-tuple-element.25), channel_id=1, source_target_pairs={{0,19},{1,4},{16,7},{17,24},{2,21},{3,6},{18,9},{19,26},{4,23},{5,... | collective-permute-start | bytes 786440 | tf_op jit(solution)/shard_map/ppermute | solution.py:197
  294.2 7.7 %collective-permute-start.20 = (bf16[16,4096]{1,0:T(8,128)(2,1)S(1)}, bf16[16,4096]{1,0:T(8,128)(2,1)S(1)}, u32[]{:S(2)}, u32[]{:S(2)}) collective-permute-start(bf16[16,4096]{1,0:T(8,128)(2,1)S(1)} %get-tuple-element.34.refs_0_), channel_id=1, source_target_pairs={{19,0},{4,1},{7,16},{24,17},{21,2},{6,3},{9,18},{26,19},{23,4},{8,... | collective-permute-start | bytes 393224 | tf_op jit(solution)/shard_map/ppermute | solution.py:188
  294.2 7.7 %collective-permute-start.19 = (bf16[16,4096]{1,0:T(8,128)(2,1)S(1)}, bf16[16,4096]{1,0:T(8,128)(2,1)S(1)}, u32[]{:S(2)}, u32[]{:S(2)}) collective-permute-start(bf16[16,4096]{1,0:T(8,128)(2,1)S(1)} %get-tuple-element.34.refs_0_), channel_id=1, source_target_pairs={{18,0},{21,1},{6,16},{9,17},{20,2},{23,3},{8,18},{11,19},{22,4},{2... | collective-permute-start | bytes 393224 | tf_op jit(solution)/shard_map/ppermute | solution.py:188
  294.2 9.4 %collective-permute-start.18 = (bf16[16,4096]{1,0:T(8,128)(2,1)S(1)}, bf16[16,4096]{1,0:T(8,128)(2,1)S(1)}, u32[]{:S(2)}, u32[]{:S(2)}) collective-permute-start(bf16[16,4096]{1,0:T(8,128)(2,1)S(1)} %get-tuple-element.34.refs_0_), channel_id=1, source_target_pairs={{3,0},{20,1},{23,16},{8,17},{5,2},{22,3},{25,18},{10,19},{7,4},{24... | collective-permute-start | bytes 393224 | tf_op jit(solution)/shard_map/ppermute | solution.py:188
  294.2 11.3 %collective-permute-start.17 = (bf16[16,4096]{1,0:T(8,128)(2,1)S(1)}, bf16[16,4096]{1,0:T(8,128)(2,1)S(1)}, u32[]{:S(2)}, u32[]{:S(2)}) collective-permute-start(bf16[16,4096]{1,0:T(8,128)(2,1)S(1)} %get-tuple-element.34.refs_0_), channel_id=1, source_target_pairs={{2,0},{5,1},{22,16},{25,17},{4,2},{7,3},{24,18},{27,19},{6,4},{9,5... | collective-permute-start | bytes 393224 | tf_op jit(solution)/shard_map/ppermute | solution.py:188
  294.3 11.2 %collective-permute-start.16 = (bf16[16,4096]{1,0:T(8,128)(2,1)S(1)}, bf16[16,4096]{1,0:T(8,128)(2,1)S(1)}, u32[]{:S(2)}, u32[]{:S(2)}) collective-permute-start(bf16[16,4096]{1,0:T(8,128)(2,1)S(1)} %get-tuple-element.34.refs_0_), channel_id=1, source_target_pairs={{17,0},{0,1},{1,16},{16,17},{19,2},{2,3},{3,18},{18,19},{21,4},{4,... | collective-permute-start | bytes 393224 | tf_op jit(solution)/shard_map/ppermute | solution.py:186
  301.9 4.7 collective-permute-start.15
  301.9 5.2 collective-permute-start.14
  517.5 24.7 %collective-permute-start.21 = (f32[16,4096]{1,0:T(8,128)S(1)}, f32[16,4096]{1,0:T(8,128)S(1)}, u32[]{:S(2)}, u32[]{:S(2)}) collective-permute-start(f32[16,4096]{1,0:T(8,128)S(1)} %get-tuple-element.27), channel_id=1, source_target_pairs={{0,1},{1,16},{16,17},{17,0},{2,3},{3,18},{18,19},{19,2},{4,5},{5,2... | collective-permute-start | bytes 786440 | tf_op jit(solution)/shard_map/ppermute | solution.py:197
  524.9 28.3 %collective-permute-start.22 = (f32[16,4096]{1,0:T(8,128)S(1)}, f32[16,4096]{1,0:T(8,128)S(1)}, u32[]{:S(2)}, u32[]{:S(2)}) collective-permute-start(f32[16,4096]{1,0:T(8,128)S(1)} %get-tuple-element.28), channel_id=1, source_target_pairs={{0,16},{1,17},{16,0},{17,1},{2,18},{3,19},{18,2},{19,3},{4,20},{5,... | collective-permute-start | bytes 786440 | tf_op jit(solution)/shard_map/ppermute | solution.py:197
  541.4 12.7 %collective-permute-start.23 = (f32[16,4096]{1,0:T(8,128)S(1)}, f32[16,4096]{1,0:T(8,128)S(1)}, u32[]{:S(2)}, u32[]{:S(2)}) collective-permute-start(f32[16,4096]{1,0:T(8,128)S(1)} %get-tuple-element.29), channel_id=1, source_target_pairs={{0,17},{1,0},{16,1},{17,16},{2,19},{3,2},{18,3},{19,18},{4,21},{5,... | collective-permute-start | bytes 786440 | tf_op jit(solution)/shard_map/ppermute | solution.py:197
  542.1 11.9 %collective-permute-start.24 = (f32[16,4096]{1,0:T(8,128)S(1)}, f32[16,4096]{1,0:T(8,128)S(1)}, u32[]{:S(2)}, u32[]{:S(2)}) collective-permute-start(f32[16,4096]{1,0:T(8,128)S(1)} %get-tuple-element.30), channel_id=1, source_target_pairs={{0,2},{1,5},{16,22},{17,25},{2,4},{3,7},{18,24},{19,27},{4,6},{5,9... | collective-permute-start | bytes 786440 | tf_op jit(solution)/shard_map/ppermute | solution.py:197
  542.1 15.3 %collective-permute-start.25 = (f32[16,4096]{1,0:T(8,128)S(1)}, f32[16,4096]{1,0:T(8,128)S(1)}, u32[]{:S(2)}, u32[]{:S(2)}) collective-permute-start(f32[16,4096]{1,0:T(8,128)S(1)} %get-tuple-element.31), channel_id=1, source_target_pairs={{0,3},{1,20},{16,23},{17,8},{2,5},{3,22},{18,25},{19,10},{4,7},{5,... | collective-permute-start | bytes 786440 | tf_op jit(solution)/shard_map/ppermute | solution.py:197
  542.1 25.3 %collective-permute-start.26 = (f32[16,4096]{1,0:T(8,128)S(1)}, f32[16,4096]{1,0:T(8,128)S(1)}, u32[]{:S(2)}, u32[]{:S(2)}) collective-permute-start(f32[16,4096]{1,0:T(8,128)S(1)} %get-tuple-element.32), channel_id=1, source_target_pairs={{0,18},{1,21},{16,6},{17,9},{2,20},{3,23},{18,8},{19,11},{4,22},{5... | collective-permute-start | bytes 786440 | tf_op jit(solution)/shard_map/ppermute | solution.py:197
  553.2 29.0 %collective-permute-start.27 = (f32[16,4096]{1,0:T(8,128)S(1)}, f32[16,4096]{1,0:T(8,128)S(1)}, u32[]{:S(2)}, u32[]{:S(2)}) collective-permute-start(f32[16,4096]{1,0:T(8,128)S(1)} %get-tuple-element.33), channel_id=1, source_target_pairs={{0,19},{1,4},{16,7},{17,24},{2,21},{3,6},{18,9},{19,26},{4,23},{5,... | collective-permute-start | bytes 786440 | tf_op jit(solution)/shard_map/ppermute | solution.py:197

commit v2 on v1

--- a/solution.py
+++ b/solution.py
@@ -12,6 +12,7 @@
 AXES = ("mirror", "rows", "cols")
 F32 = jnp.float32
 BF16 = jnp.bfloat16
+SENT = (BF16, BF16)
 SUB = 256
 STRIP = 16
 LAST = (((1,), (1,)), ((), ()))
@@ -155,10 +156,10 @@
         half, offset = place(index)
         rows = pl.ds(pl.multiple_of(half * 16, 16), 16)
         cols = pl.ds(offset, piece_len)
-        results[index][...] = by_column[rows, cols] + by_row[rows, cols]
-
-
-def apply_operator(plan, table, counts, geo, pieces):
+        results[index][...] = (by_column[rows, cols] + by_row[rows, cols]).astype(results[index].dtype)
+
+
+def apply_operator(plan, table, counts, geo, pieces, sent):
     cells = 2 * plan.block_len
     vmem = pl.BlockSpec(memory_space=pltpu.VMEM)
     smem = pl.BlockSpec(memory_space=pltpu.SMEM)
@@ -166,7 +167,9 @@
         functools.partial(operator_kernel, plan),
         in_specs=[smem, smem, vmem] + [vmem] * plan.blocks,
         out_specs=[vmem] * plan.blocks,
-        out_shape=[jax.ShapeDtypeStruct((16, plan.piece_len), F32)] * plan.blocks,
+        out_shape=[
+            jax.ShapeDtypeStruct((16, plan.piece_len), sent if index else F32) for index in range(plan.blocks)
+        ],
         scratch_shapes=[
             pltpu.VMEM((64, cells), BF16),
             pltpu.VMEM((32, cells), F32),
@@ -194,7 +197,7 @@
     for index in range(1, plan.blocks):
         route = plan.route(index < plan.homes, index % plan.homes)
         back = [(target, source) for source, target in route]
-        total = total + lax.ppermute(partials[index], AXES, back)
+        total = total + lax.ppermute(partials[index], AXES, back).astype(F32)
     return total
 
 
@@ -227,9 +230,10 @@
     geo = local_geometry(plan, geometry, block, partner)
 
     own = lax.dynamic_slice_in_dim(currents, lax.axis_index("cols") * plan.piece_len, plan.piece_len, 1)
-    partials = apply_operator(plan, table, counts, geo, gather_pieces(plan, own))
+    partials = apply_operator(plan, table, counts, geo, gather_pieces(plan, own), SENT[0])
     residual = right_side - return_pieces(plan, partials)
-    partials = apply_operator(plan, table, counts, geo, gather_pieces(plan, residual.astype(BF16)))
+    pieces = gather_pieces(plan, residual.astype(BF16))
+    partials = apply_operator(plan, table, counts, geo, pieces, SENT[1])
     return residual, return_pieces(plan, partials)
 
 

time: 583 us -> 543 us (0.931)
  waiting for transfers between devices: 92.7 us -> 60.1 us
  starting transfers between devices: 64.1 us -> 56.5 us
    ppermute x14, waiting for transfers between devices: 80.1 us -> 43.1 us  [return_pieces(): total = total + lax.ppermute(partials[index], AXES, back).astype(F32)]
  transfers between devices with their start and end apart: 28 -> 28, of which waited for: 17 -> 18; matrix products, arithmetic and copies ran while one was open for 0% -> 0% of each run, Pallas kernels for 0% -> 0%
where the time goes in v2:
time: 543 us
  Pallas kernels  420 us (77%)
  waiting for transfers between devices  60.1 us (11%)
  starting transfers between devices  56.5 us (10%)
    pallas_call x2, Pallas kernels, apply_operator(): pl.pallas_call(functools.partial(operator_kernel, plan), in_specs=[smem,...  420 us
    ppermute x14, waiting for transfers between devices, return_pieces(): total = total + lax.ppermute(partials[index], AXES, back).astype(F32)  43.1 us
    ppermute x14, starting transfers between devices, return_pieces(): total = total + lax.ppermute(partials[index], AXES, back).astype(F32)  38.1 us
    ppermute x6, starting transfers between devices, gather_pieces(): pieces.append(lax.ppermute(own, AXES, plan.route(True, step)))  11.2 us
  transfers between devices with their start and end apart: 28, of which 18 were waited for; matrix products, arithmetic and copies ran while one was open for 0% of the time, Pallas kernels for 0%

profile of v2, /device:TPU:25, one launch (start us, length us, event | category | flops | bytes accessed | tf_op | source)
XLA Modules:
  0.0 542.8 jit_solution(1641622068239849188)
XLA Ops:
  0.6 1.0 copy-done
  1.7 2.6 collective-permute-start.6
  4.4 2.5 collective-permute-start.4
  6.8 0.9 collective-permute-start.3
  7.7 1.8 collective-permute-start.2
  9.5 1.0 constant_dynamic-slice_fusion.2
  10.9 9.4 %collective-permute-start.1 = (bf16[16,4096]{1,0:T(8,128)(2,1)S(1)}, bf16[16,4096]{1,0:T(8,128)(2,1)S(1)}, u32[]{:S(2)}, u32[]{:S(2)}) collective-permute-start(bf16[16,4096]{1,0:T(8,128)(2,1)S(1)} %constant_dynamic-slice_fusion.refs_0_), channel_id=1, source_target_pairs={{16,0},{17,1},{0,16},{1,17},{18,2},{19,3},{2,18},{3,19},{20,4},{21... | collective-permute-start | bytes 393224 | tf_op jit(solution)/shard_map/ppermute | solution.py:189
  20.4 0.7 stack.28.geo
  21.2 2.8 collective-permute-done.1.refs_2_
  24.7 210.1 %peec_pairs.2 = (f32[16,4096]{1,0:T(8,128)S(1)}, bf16[16,4096]{1,0:T(8,128)(2,1)S(1)}, bf16[16,4096]{1,0:T(8,128)(2,1)S(1)}, bf16[16,4096]{1,0:T(8,128)(2,1)S(1)...) custom-call(s32[3,65]{1,0:T(4,128)S(1)} %broadcast_select_fusion.tab, ...), custom_call_target="tpu_custom_call" | custom-call | tf_op jit(solution)/shard_map/peec_pairs/pallas_call | solution.py:166
  234.7 1.2 collective-permute-start.7
  236.0 16.5 %collective-permute-start.8 = (bf16[16,4096]{1,0:T(8,128)(2,1)S(1)}, bf16[16,4096]{1,0:T(8,128)(2,1)S(1)}, u32[]{:S(2)}, u32[]{:S(2)}) collective-permute-start(bf16[16,4096]{1,0:T(8,128)(2,1)S(1)} %get-tuple-element.20), channel_id=1, source_target_pairs={{0,16},{1,17},{16,0},{17,1},{2,18},{3,19},{18,2},{19,3},{4,20},{5,... | collective-permute-start | bytes 393224 | tf_op jit(solution)/shard_map/ppermute | solution.py:200
  253.2 6.8 %collective-permute-done.8 = bf16[16,4096]{1,0:T(8,128)(2,1)S(1)} collective-permute-done((bf16[16,4096]{1,0:T(8,128)(2,1)S(1)}, bf16[16,4096]{1,0:T(8,128)(2,1)S(1)}, u32[]{:S(2)}, u32[]{:S(2)}) %collective-permute-start.8) | collective-permute-done | bytes 131104 | tf_op jit(solution)/shard_map/ppermute | solution.py:200
  260.7 1.8 collective-permute-done.11
  262.6 2.2 collective-permute-done.12
  264.8 9.4 %collective-permute-done.13 = bf16[16,4096]{1,0:T(8,128)(2,1)S(1)} collective-permute-done((bf16[16,4096]{1,0:T(8,128)(2,1)S(1)}, bf16[16,4096]{1,0:T(8,128)(2,1)S(1)}, u32[]{:S(2)}, u32[]{:S(2)}) %collective-permute-start.13) | collective-permute-done | bytes 131104 | tf_op jit(solution)/shard_map/ppermute | solution.py:200
  274.2 0.9 fusion.8
  275.1 1.3 collective-permute-start.18
  276.4 5.7 %collective-permute-done.20.refs_7_ = bf16[16,4096]{1,0:T(8,128)(2,1)S(1)} collective-permute-done((bf16[16,4096]{1,0:T(8,128)(2,1)S(1)}, bf16[16,4096]{1,0:T(8,128)(2,1)S(1)}, u32[]{:S(2)}, u32[]{:S(2)}) %collective-permute-start.20) | collective-permute-done | bytes 131104 | tf_op jit(solution)/shard_map/ppermute | solution.py:191
  282.1 1.8 collective-permute-done.19.refs_6_
  284.5 1.9 collective-permute-done.17.refs_4_
  286.3 2.1 collective-permute-done.15.refs_2_
  288.4 1.5 collective-permute-done.14.refs_1_
  290.0 210.3 %peec_pairs.3 = (f32[16,4096]{1,0:T(8,128)S(1)}, bf16[16,4096]{1,0:T(8,128)(2,1)S(1)}, bf16[16,4096]{1,0:T(8,128)(2,1)S(1)}, bf16[16,4096]{1,0:T(8,128)(2,1)S(1)...) custom-call(s32[3,65]{1,0:T(4,128)S(1)} %broadcast_select_fusion.tab, ...), custom_call_target="tpu_custom_call" | custom-call | tf_op jit(solution)/shard_map/peec_pairs/pallas_call | solution.py:166
  500.2 2.3 collective-permute-start.21
  502.6 16.5 %collective-permute-start.22 = (bf16[16,4096]{1,0:T(8,128)(2,1)S(1)}, bf16[16,4096]{1,0:T(8,128)(2,1)S(1)}, u32[]{:S(2)}, u32[]{:S(2)}) collective-permute-start(bf16[16,4096]{1,0:T(8,128)(2,1)S(1)} %get-tuple-element.28), channel_id=1, source_target_pairs={{0,16},{1,17},{16,0},{17,1},{2,18},{3,19},{18,2},{19,3},{4,20},{5,... | collective-permute-start | bytes 393224 | tf_op jit(solution)/shard_map/ppermute | solution.py:200
  519.8 5.3 collective-permute-done.22
  525.2 1.7 collective-permute-done.23
  526.9 2.3 collective-permute-done.25
  529.2 3.1 collective-permute-done.26
  532.3 9.7 %collective-permute-done.27 = bf16[16,4096]{1,0:T(8,128)(2,1)S(1)} collective-permute-done((bf16[16,4096]{1,0:T(8,128)(2,1)S(1)}, bf16[16,4096]{1,0:T(8,128)(2,1)S(1)}, u32[]{:S(2)}, u32[]{:S(2)}) %collective-permute-start.27) | collective-permute-done | bytes 131104 | tf_op jit(solution)/shard_map/ppermute | solution.py:200
  542.0 0.8 convert_add_fusion
  (45 shorter events, 4.1 us)
Async XLA Ops:
  0.6 1.0 copy-start
  1.7 9.2 %collective-permute-start.6 = (bf16[16,4096]{1,0:T(8,128)(2,1)S(1)}, bf16[16,4096]{1,0:T(8,128)(2,1)S(1)}, u32[]{:S(2)}, u32[]{:S(2)}) collective-permute-start(bf16[16,4096]{1,0:T(8,128)(2,1)S(1)} %constant_dynamic-slice_fusion.refs_0_), channel_id=1, source_target_pairs={{19,0},{4,1},{7,16},{24,17},{21,2},{6,3},{9,18},{26,19},{23,4},{8,... | collective-permute-start | bytes 393224 | tf_op jit(solution)/shard_map/ppermute | solution.py:191
  4.2 16.0 %collective-permute-start.5 = (bf16[16,4096]{1,0:T(8,128)(2,1)S(1)}, bf16[16,4096]{1,0:T(8,128)(2,1)S(1)}, u32[]{:S(2)}, u32[]{:S(2)}) collective-permute-start(bf16[16,4096]{1,0:T(8,128)(2,1)S(1)} %constant_dynamic-slice_fusion.refs_0_), channel_id=1, source_target_pairs={{18,0},{21,1},{6,16},{9,17},{20,2},{23,3},{8,18},{11,19},{22,4},{2... | collective-permute-start | bytes 393224 | tf_op jit(solution)/shard_map/ppermute | solution.py:191
  4.4 16.9 %collective-permute-start.4 = (bf16[16,4096]{1,0:T(8,128)(2,1)S(1)}, bf16[16,4096]{1,0:T(8,128)(2,1)S(1)}, u32[]{:S(2)}, u32[]{:S(2)}) collective-permute-start(bf16[16,4096]{1,0:T(8,128)(2,1)S(1)} %constant_dynamic-slice_fusion.refs_0_), channel_id=1, source_target_pairs={{3,0},{20,1},{23,16},{8,17},{5,2},{22,3},{25,18},{10,19},{7,4},{24... | collective-permute-start | bytes 393224 | tf_op jit(solution)/shard_map/ppermute | solution.py:191
  6.8 14.4 %collective-permute-start.3 = (bf16[16,4096]{1,0:T(8,128)(2,1)S(1)}, bf16[16,4096]{1,0:T(8,128)(2,1)S(1)}, u32[]{:S(2)}, u32[]{:S(2)}) collective-permute-start(bf16[16,4096]{1,0:T(8,128)(2,1)S(1)} %constant_dynamic-slice_fusion.refs_0_), channel_id=1, source_target_pairs={{2,0},{5,1},{22,16},{25,17},{4,2},{7,3},{24,18},{27,19},{6,4},{9,5... | collective-permute-start | bytes 393224 | tf_op jit(solution)/shard_map/ppermute | solution.py:191
  7.7 13.6 %collective-permute-start.2 = (bf16[16,4096]{1,0:T(8,128)(2,1)S(1)}, bf16[16,4096]{1,0:T(8,128)(2,1)S(1)}, u32[]{:S(2)}, u32[]{:S(2)}) collective-permute-start(bf16[16,4096]{1,0:T(8,128)(2,1)S(1)} %constant_dynamic-slice_fusion.refs_0_), channel_id=1, source_target_pairs={{17,0},{0,1},{1,16},{16,17},{19,2},{2,3},{3,18},{18,19},{21,4},{4,... | collective-permute-start | bytes 393224 | tf_op jit(solution)/shard_map/ppermute | solution.py:189
  10.9 9.4 %copy-start.3 = (s32[3,65]{1,0:T(4,128)S(1)}, s32[3,65]{1,0:T(4,128)}, u32[]{:S(2)}) copy-start(s32[3,65]{1,0:T(4,128)} %constant.76.clone) | copy-start | bytes 2344
  10.9 9.4 %copy-start.2 = (s32[3,65]{1,0:T(4,128)S(1)}, s32[3,65]{1,0:T(4,128)}, u32[]{:S(2)}) copy-start(s32[3,65]{1,0:T(4,128)} %constant.77.clone) | copy-start | bytes 2344
  10.9 13.2 %collective-permute-start.1 = (bf16[16,4096]{1,0:T(8,128)(2,1)S(1)}, bf16[16,4096]{1,0:T(8,128)(2,1)S(1)}, u32[]{:S(2)}, u32[]{:S(2)}) collective-permute-start(bf16[16,4096]{1,0:T(8,128)(2,1)S(1)} %constant_dynamic-slice_fusion.refs_0_), channel_id=1, source_target_pairs={{16,0},{17,1},{0,16},{1,17},{18,2},{19,3},{2,18},{3,19},{20,4},{21... | collective-permute-start | bytes 393224 | tf_op jit(solution)/shard_map/ppermute | solution.py:189
  20.3 4.4 collective-permute-start
  21.2 253.0 %copy-start.1 = (f32[16,4096]{1,0:T(8,128)S(1)}, f32[16,4096]{1,0:T(8,128)}, u32[]{:S(2)}) copy-start(f32[16,4096]{1,0:T(8,128)} %param.6) | copy-start | bytes 786436
  234.7 18.4 %collective-permute-start.7 = (bf16[16,4096]{1,0:T(8,128)(2,1)S(1)}, bf16[16,4096]{1,0:T(8,128)(2,1)S(1)}, u32[]{:S(2)}, u32[]{:S(2)}) collective-permute-start(bf16[16,4096]{1,0:T(8,128)(2,1)S(1)} %get-tuple-element.19), channel_id=1, source_target_pairs={{0,1},{1,16},{16,17},{17,0},{2,3},{3,18},{18,19},{19,2},{4,5},{5,2... | collective-permute-start | bytes 393224 | tf_op jit(solution)/shard_map/ppermute | solution.py:200
  236.0 24.1 %collective-permute-start.8 = (bf16[16,4096]{1,0:T(8,128)(2,1)S(1)}, bf16[16,4096]{1,0:T(8,128)(2,1)S(1)}, u32[]{:S(2)}, u32[]{:S(2)}) collective-permute-start(bf16[16,4096]{1,0:T(8,128)(2,1)S(1)} %get-tuple-element.20), channel_id=1, source_target_pairs={{0,16},{1,17},{16,0},{17,1},{2,18},{3,19},{18,2},{19,3},{4,20},{5,... | collective-permute-start | bytes 393224 | tf_op jit(solution)/shard_map/ppermute | solution.py:200
  252.4 8.3 %collective-permute-start.9 = (bf16[16,4096]{1,0:T(8,128)(2,1)S(1)}, bf16[16,4096]{1,0:T(8,128)(2,1)S(1)}, u32[]{:S(2)}, u32[]{:S(2)}) collective-permute-start(bf16[16,4096]{1,0:T(8,128)(2,1)S(1)} %get-tuple-element.21), channel_id=1, source_target_pairs={{0,17},{1,0},{16,1},{17,16},{2,19},{3,2},{18,3},{19,18},{4,21},{5,... | collective-permute-start | bytes 393224 | tf_op jit(solution)/shard_map/ppermute | solution.py:200
  253.2 7.6 %collective-permute-start.10 = (bf16[16,4096]{1,0:T(8,128)(2,1)S(1)}, bf16[16,4096]{1,0:T(8,128)(2,1)S(1)}, u32[]{:S(2)}, u32[]{:S(2)}) collective-permute-start(bf16[16,4096]{1,0:T(8,128)(2,1)S(1)} %get-tuple-element.22), channel_id=1, source_target_pairs={{0,2},{1,5},{16,22},{17,25},{2,4},{3,7},{18,24},{19,27},{4,6},{5,9... | collective-permute-start | bytes 393224 | tf_op jit(solution)/shard_map/ppermute | solution.py:200
  253.2 9.4 %collective-permute-start.11 = (bf16[16,4096]{1,0:T(8,128)(2,1)S(1)}, bf16[16,4096]{1,0:T(8,128)(2,1)S(1)}, u32[]{:S(2)}, u32[]{:S(2)}) collective-permute-start(bf16[16,4096]{1,0:T(8,128)(2,1)S(1)} %get-tuple-element.23), channel_id=1, source_target_pairs={{0,3},{1,20},{16,23},{17,8},{2,5},{3,22},{18,25},{19,10},{4,7},{5,... | collective-permute-start | bytes 393224 | tf_op jit(solution)/shard_map/ppermute | solution.py:200
  253.2 11.6 %collective-permute-start.12 = (bf16[16,4096]{1,0:T(8,128)(2,1)S(1)}, bf16[16,4096]{1,0:T(8,128)(2,1)S(1)}, u32[]{:S(2)}, u32[]{:S(2)}) collective-permute-start(bf16[16,4096]{1,0:T(8,128)(2,1)S(1)} %get-tuple-element.24), channel_id=1, source_target_pairs={{0,18},{1,21},{16,6},{17,9},{2,20},{3,23},{18,8},{19,11},{4,22},{5... | collective-permute-start | bytes 393224 | tf_op jit(solution)/shard_map/ppermute | solution.py:200
  260.1 14.1 %collective-permute-start.13 = (bf16[16,4096]{1,0:T(8,128)(2,1)S(1)}, bf16[16,4096]{1,0:T(8,128)(2,1)S(1)}, u32[]{:S(2)}, u32[]{:S(2)}) collective-permute-start(bf16[16,4096]{1,0:T(8,128)(2,1)S(1)} %get-tuple-element.25), channel_id=1, source_target_pairs={{0,19},{1,4},{16,7},{17,24},{2,21},{3,6},{18,9},{19,26},{4,23},{5,... | collective-permute-start | bytes 393224 | tf_op jit(solution)/shard_map/ppermute | solution.py:200
  275.1 7.0 %collective-permute-start.20 = (bf16[16,4096]{1,0:T(8,128)(2,1)S(1)}, bf16[16,4096]{1,0:T(8,128)(2,1)S(1)}, u32[]{:S(2)}, u32[]{:S(2)}) collective-permute-start(bf16[16,4096]{1,0:T(8,128)(2,1)S(1)} %get-tuple-element.34.refs_0_), channel_id=1, source_target_pairs={{19,0},{4,1},{7,16},{24,17},{21,2},{6,3},{9,18},{26,19},{23,4},{8,... | collective-permute-start | bytes 393224 | tf_op jit(solution)/shard_map/ppermute | solution.py:191
  275.1 8.8 %collective-permute-start.19 = (bf16[16,4096]{1,0:T(8,128)(2,1)S(1)}, bf16[16,4096]{1,0:T(8,128)(2,1)S(1)}, u32[]{:S(2)}, u32[]{:S(2)}) collective-permute-start(bf16[16,4096]{1,0:T(8,128)(2,1)S(1)} %get-tuple-element.34.refs_0_), channel_id=1, source_target_pairs={{18,0},{21,1},{6,16},{9,17},{20,2},{23,3},{8,18},{11,19},{22,4},{2... | collective-permute-start | bytes 393224 | tf_op jit(solution)/shard_map/ppermute | solution.py:191
  275.1 9.4 %collective-permute-start.18 = (bf16[16,4096]{1,0:T(8,128)(2,1)S(1)}, bf16[16,4096]{1,0:T(8,128)(2,1)S(1)}, u32[]{:S(2)}, u32[]{:S(2)}) collective-permute-start(bf16[16,4096]{1,0:T(8,128)(2,1)S(1)} %get-tuple-element.34.refs_0_), channel_id=1, source_target_pairs={{3,0},{20,1},{23,16},{8,17},{5,2},{22,3},{25,18},{10,19},{7,4},{24... | collective-permute-start | bytes 393224 | tf_op jit(solution)/shard_map/ppermute | solution.py:191
  276.4 10.0 %collective-permute-start.17 = (bf16[16,4096]{1,0:T(8,128)(2,1)S(1)}, bf16[16,4096]{1,0:T(8,128)(2,1)S(1)}, u32[]{:S(2)}, u32[]{:S(2)}) collective-permute-start(bf16[16,4096]{1,0:T(8,128)(2,1)S(1)} %get-tuple-element.34.refs_0_), channel_id=1, source_target_pairs={{2,0},{5,1},{22,16},{25,17},{4,2},{7,3},{24,18},{27,19},{6,4},{9,5... | collective-permute-start | bytes 393224 | tf_op jit(solution)/shard_map/ppermute | solution.py:191
  276.4 10.0 %collective-permute-start.16 = (bf16[16,4096]{1,0:T(8,128)(2,1)S(1)}, bf16[16,4096]{1,0:T(8,128)(2,1)S(1)}, u32[]{:S(2)}, u32[]{:S(2)}) collective-permute-start(bf16[16,4096]{1,0:T(8,128)(2,1)S(1)} %get-tuple-element.34.refs_0_), channel_id=1, source_target_pairs={{17,0},{0,1},{1,16},{16,17},{19,2},{2,3},{3,18},{18,19},{21,4},{4,... | collective-permute-start | bytes 393224 | tf_op jit(solution)/shard_map/ppermute | solution.py:189
  282.1 6.4 %collective-permute-start.15 = (bf16[16,4096]{1,0:T(8,128)(2,1)S(1)}, bf16[16,4096]{1,0:T(8,128)(2,1)S(1)}, u32[]{:S(2)}, u32[]{:S(2)}) collective-permute-start(bf16[16,4096]{1,0:T(8,128)(2,1)S(1)} %get-tuple-element.34.refs_0_), channel_id=1, source_target_pairs={{16,0},{17,1},{0,16},{1,17},{18,2},{19,3},{2,18},{3,19},{20,4},{21... | collective-permute-start | bytes 393224 | tf_op jit(solution)/shard_map/ppermute | solution.py:189
  283.9 6.1 %collective-permute-start.14 = (bf16[16,4096]{1,0:T(8,128)(2,1)S(1)}, bf16[16,4096]{1,0:T(8,128)(2,1)S(1)}, u32[]{:S(2)}, u32[]{:S(2)}) collective-permute-start(bf16[16,4096]{1,0:T(8,128)(2,1)S(1)} %get-tuple-element.34.refs_0_), channel_id=1, source_target_pairs={{1,0},{16,1},{17,16},{0,17},{3,2},{18,3},{19,18},{2,19},{5,4},{20,... | collective-permute-start | bytes 393224 | tf_op jit(solution)/shard_map/ppermute | solution.py:189
  500.2 19.5 %collective-permute-start.21 = (bf16[16,4096]{1,0:T(8,128)(2,1)S(1)}, bf16[16,4096]{1,0:T(8,128)(2,1)S(1)}, u32[]{:S(2)}, u32[]{:S(2)}) collective-permute-start(bf16[16,4096]{1,0:T(8,128)(2,1)S(1)} %get-tuple-element.27), channel_id=1, source_target_pairs={{0,1},{1,16},{16,17},{17,0},{2,3},{3,18},{18,19},{19,2},{4,5},{5,2... | collective-permute-start | bytes 393224 | tf_op jit(solution)/shard_map/ppermute | solution.py:200
  502.6 22.6 %collective-permute-start.22 = (bf16[16,4096]{1,0:T(8,128)(2,1)S(1)}, bf16[16,4096]{1,0:T(8,128)(2,1)S(1)}, u32[]{:S(2)}, u32[]{:S(2)}) collective-permute-start(bf16[16,4096]{1,0:T(8,128)(2,1)S(1)} %get-tuple-element.28), channel_id=1, source_target_pairs={{0,16},{1,17},{16,0},{17,1},{2,18},{3,19},{18,2},{19,3},{4,20},{5,... | collective-permute-start | bytes 393224 | tf_op jit(solution)/shard_map/ppermute | solution.py:200
  519.1 7.8 %collective-permute-start.23 = (bf16[16,4096]{1,0:T(8,128)(2,1)S(1)}, bf16[16,4096]{1,0:T(8,128)(2,1)S(1)}, u32[]{:S(2)}, u32[]{:S(2)}) collective-permute-start(bf16[16,4096]{1,0:T(8,128)(2,1)S(1)} %get-tuple-element.29), channel_id=1, source_target_pairs={{0,17},{1,0},{16,1},{17,16},{2,19},{3,2},{18,3},{19,18},{4,21},{5,... | collective-permute-start | bytes 393224 | tf_op jit(solution)/shard_map/ppermute | solution.py:200
  519.8 7.1 %collective-permute-start.24 = (bf16[16,4096]{1,0:T(8,128)(2,1)S(1)}, bf16[16,4096]{1,0:T(8,128)(2,1)S(1)}, u32[]{:S(2)}, u32[]{:S(2)}) collective-permute-start(bf16[16,4096]{1,0:T(8,128)(2,1)S(1)} %get-tuple-element.30), channel_id=1, source_target_pairs={{0,2},{1,5},{16,22},{17,25},{2,4},{3,7},{18,24},{19,27},{4,6},{5,9... | collective-permute-start | bytes 393224 | tf_op jit(solution)/shard_map/ppermute | solution.py:200
  519.8 9.4 %collective-permute-start.25 = (bf16[16,4096]{1,0:T(8,128)(2,1)S(1)}, bf16[16,4096]{1,0:T(8,128)(2,1)S(1)}, u32[]{:S(2)}, u32[]{:S(2)}) collective-permute-start(bf16[16,4096]{1,0:T(8,128)(2,1)S(1)} %get-tuple-element.31), channel_id=1, source_target_pairs={{0,3},{1,20},{16,23},{17,8},{2,5},{3,22},{18,25},{19,10},{4,7},{5,... | collective-permute-start | bytes 393224 | tf_op jit(solution)/shard_map/ppermute | solution.py:200
  519.8 12.5 %collective-permute-start.26 = (bf16[16,4096]{1,0:T(8,128)(2,1)S(1)}, bf16[16,4096]{1,0:T(8,128)(2,1)S(1)}, u32[]{:S(2)}, u32[]{:S(2)}) collective-permute-start(bf16[16,4096]{1,0:T(8,128)(2,1)S(1)} %get-tuple-element.32), channel_id=1, source_target_pairs={{0,18},{1,21},{16,6},{17,9},{2,20},{3,23},{18,8},{19,11},{4,22},{5... | collective-permute-start | bytes 393224 | tf_op jit(solution)/shard_map/ppermute | solution.py:200
  525.2 16.8 %collective-permute-start.27 = (bf16[16,4096]{1,0:T(8,128)(2,1)S(1)}, bf16[16,4096]{1,0:T(8,128)(2,1)S(1)}, u32[]{:S(2)}, u32[]{:S(2)}) collective-permute-start(bf16[16,4096]{1,0:T(8,128)(2,1)S(1)} %get-tuple-element.33), channel_id=1, source_target_pairs={{0,19},{1,4},{16,7},{17,24},{2,21},{3,6},{18,9},{19,26},{4,23},{5,... | collective-permute-start | bytes 393224 | tf_op jit(solution)/shard_map/ppermute | solution.py:200

commit v3 on v2

--- a/solution.py
+++ b/solution.py
@@ -50,9 +50,9 @@
         ]
         tables = []
         for work in (pair, diagonal):
-            table = np.zeros((3, count * count + 1), np.int32)
-            for at, (i, j) in enumerate(work):
-                table[:, at] = i, j, at == 0 or work[at - 1][0] != i
+            table = np.zeros((2, count * count + 1), np.int32)
+            for at, place in enumerate(work):
+                table[:, at] = place
             tables.append(table)
         return tables[0], tables[1], len(pair), len(diagonal)
 
@@ -79,12 +79,14 @@
     by_column[...] = jnp.zeros_like(by_column)
     by_row[...] = jnp.zeros_like(by_row)
 
-    def turn(row0):
+    def turn(at, carry):
+        row0 = pl.multiple_of(at * tile, tile)
         for part in range(tile // 128):
-            turned[part * 128 : part * 128 + 128, :] = jnp.transpose(geo[:, pl.ds(row0 + part * 128, 128)])
-
-    def make(slot, row, col0, first, at, lanes=0):
-        part = turned[row : row + STRIP, :]
+            turned[pl.ds(row0 + part * 128, 128), :] = jnp.transpose(geo[:, pl.ds(row0 + part * 128, 128)])
+        return carry
+
+    def make(slot, row, col0, at, lanes=0):
+        part = turned[pl.ds(row, STRIP), :]
         x_r, y_r, z_r, q_r = [jnp.broadcast_to(part[:, n : n + 1], (STRIP, 128)) for n in range(4)]
         for lane in range(lanes, tile, 128):
             cols = geo[:, pl.ds(col0 + lane, 128)]
@@ -112,20 +114,15 @@
     def pair_tile(at, carry):
         row0 = pl.multiple_of(table[0, at] * tile, tile)
         col0 = pl.multiple_of(table[1, at] * tile, tile)
-        next0 = pl.multiple_of(table[1, at + 1] * tile, tile)
-
-        @pl.when(table[2, at] == 1)
-        def _():
-            turn(row0)
-            for strip in range(strips):
-                make(0, strip * STRIP, col0, True, strip * STRIP)
-
+        next_row0 = pl.multiple_of(table[0, at + 1] * tile, tile)
+        next_col0 = pl.multiple_of(table[1, at + 1] * tile, tile)
         for sub in range(chunks):
-            ahead, ahead0 = (sub + 1, col0) if sub + 1 < chunks else (0, next0)
+            inside = sub + 1 < chunks
+            ahead_row, ahead_col = (row0 + (sub + 1) * SUB, col0) if inside else (next_row0, next_col0)
             total = None
             for chunk in range(chunks):
                 for strip in range(chunk * strips // chunks, (chunk + 1) * strips // chunks):
-                    make((sub + 1) % 2, ahead * SUB + strip * STRIP, ahead0, False, strip * STRIP)
+                    make((sub + 1) % 2, ahead_row + strip * STRIP, ahead_col, strip * STRIP)
                 to_columns(sub % 2, row0 + sub * SUB, col0, chunk)
                 term = to_rows(sub % 2, col0, chunk)
                 total = term if total is None else total + term
@@ -134,11 +131,10 @@
 
     def diagonal_tile(at, carry):
         row0 = pl.multiple_of(at * tile, tile)
-        turn(row0)
         for sub in range(chunks):
             slot = sub % 2
             for strip in range(strips):
-                make(slot, sub * SUB + strip * STRIP, row0, False, strip * STRIP, sub * SUB)
+                make(slot, row0 + sub * SUB + strip * STRIP, row0, strip * STRIP, sub * SUB)
             total = None
             for chunk in range(sub, chunks):
                 to_columns(slot, row0 + sub * SUB, row0, chunk)
@@ -149,6 +145,11 @@
                 by_row[:, pl.ds(row0 + sub * SUB, SUB)] += total
         return carry
 
+    lax.fori_loop(0, jnp.maximum(plan.tiles, counts[1]), turn, 0)
+    first_row = pl.multiple_of(table[0, 0] * tile, tile)
+    first_col = pl.multiple_of(table[1, 0] * tile, tile)
+    for strip in range(strips):
+        make(0, first_row + strip * STRIP, first_col, strip * STRIP)
     lax.fori_loop(0, counts[0], pair_tile, 0)
     lax.fori_loop(0, counts[1], diagonal_tile, 0)
 
@@ -176,7 +177,7 @@
             pltpu.VMEM((32, cells), F32),
             pltpu.VMEM((2, SUB, plan.tile), BF16),
             pltpu.VMEM((2, SUB, plan.tile), BF16),
-            pltpu.VMEM((plan.tile, 8), F32),
+            pltpu.VMEM((cells, 8), F32),
         ],
         compiler_params=pltpu.CompilerParams(vmem_limit_bytes=40 * 2**20),
         name="peec_pairs",

time: 543 us -> 520 us (0.958)
  starting transfers between devices: 56.5 us -> 41.8 us
  Pallas kernels: 420 us -> 412 us
    ppermute x14, starting transfers between devices: 38.1 us -> 23.4 us  [return_pieces(): total = total + lax.ppermute(partials[index], AXES, back).astype(F32)]
    pallas_call x2, Pallas kernels: 420 us -> 412 us  [apply_operator(): pl.pallas_call(functools.partial(operator_kernel, plan), in_specs=[smem,...]
where the time goes in v3:
time: 520 us
  Pallas kernels  412 us (79%)
  waiting for transfers between devices  60.1 us (12%)
  starting transfers between devices  41.8 us (8%)
    pallas_call x2, Pallas kernels, apply_operator(): pl.pallas_call(functools.partial(operator_kernel, plan), in_specs=[smem,...  412 us
    ppermute x14, waiting for transfers between devices, return_pieces(): total = total + lax.ppermute(partials[index], AXES, back).astype(F32)  43.1 us
    ppermute x14, starting transfers between devices, return_pieces(): total = total + lax.ppermute(partials[index], AXES, back).astype(F32)  23.4 us
    ppermute x6, starting transfers between devices, gather_pieces(): pieces.append(lax.ppermute(own, AXES, plan.route(True, step)))  11.2 us
  transfers between devices with their start and end apart: 28, of which 18 were waited for; matrix products, arithmetic and copies ran while one was open for 0% of the time, Pallas kernels for 0%

profile of v3, /device:TPU:25, one launch (start us, length us, event | category | flops | bytes accessed | tf_op | source)
XLA Modules:
  0.0 520.1 jit_solution(12082113328955465068)
XLA Ops:
  0.6 1.0 copy-done
  1.7 2.6 collective-permute-start.6
  4.4 2.5 collective-permute-start.4
  6.8 0.9 collective-permute-start.3
  7.7 1.8 collective-permute-start.2
  9.5 1.0 constant_dynamic-slice_fusion.2
  10.9 9.4 %collective-permute-start.1 = (bf16[16,4096]{1,0:T(8,128)(2,1)S(1)}, bf16[16,4096]{1,0:T(8,128)(2,1)S(1)}, u32[]{:S(2)}, u32[]{:S(2)}) collective-permute-start(bf16[16,4096]{1,0:T(8,128)(2,1)S(1)} %constant_dynamic-slice_fusion.refs_0_), channel_id=1, source_target_pairs={{16,0},{17,1},{0,16},{1,17},{18,2},{19,3},{2,18},{3,19},{20,4},{21... | collective-permute-start | bytes 393224 | tf_op jit(solution)/shard_map/ppermute | solution.py:190
  20.4 0.7 stack.28.geo
  21.2 2.8 collective-permute-done.1.refs_2_
  24.7 206.1 %peec_pairs.2 = (f32[16,4096]{1,0:T(8,128)S(1)}, bf16[16,4096]{1,0:T(8,128)(2,1)S(1)}, bf16[16,4096]{1,0:T(8,128)(2,1)S(1)}, bf16[16,4096]{1,0:T(8,128)(2,1)S(1)...) custom-call(s32[2,65]{1,0:T(2,128)S(1)} %broadcast_select_fusion.tab, ...), custom_call_target="tpu_custom_call" | custom-call | tf_op jit(solution)/shard_map/peec_pairs/pallas_call | solution.py:167
  230.7 1.2 collective-permute-start.7
  232.0 9.1 %collective-permute-start.8 = (bf16[16,4096]{1,0:T(8,128)(2,1)S(1)}, bf16[16,4096]{1,0:T(8,128)(2,1)S(1)}, u32[]{:S(2)}, u32[]{:S(2)}) collective-permute-start(bf16[16,4096]{1,0:T(8,128)(2,1)S(1)} %get-tuple-element.20), channel_id=1, source_target_pairs={{0,16},{1,17},{16,0},{17,1},{2,18},{3,19},{18,2},{19,3},{4,20},{5,... | collective-permute-start | bytes 393224 | tf_op jit(solution)/shard_map/ppermute | solution.py:201
  241.9 6.8 %collective-permute-done.8 = bf16[16,4096]{1,0:T(8,128)(2,1)S(1)} collective-permute-done((bf16[16,4096]{1,0:T(8,128)(2,1)S(1)}, bf16[16,4096]{1,0:T(8,128)(2,1)S(1)}, u32[]{:S(2)}, u32[]{:S(2)}) %collective-permute-start.8) | collective-permute-done | bytes 131104 | tf_op jit(solution)/shard_map/ppermute | solution.py:201
  249.4 1.9 collective-permute-done.11
  251.2 2.2 collective-permute-done.12
  253.4 9.4 %collective-permute-done.13 = bf16[16,4096]{1,0:T(8,128)(2,1)S(1)} collective-permute-done((bf16[16,4096]{1,0:T(8,128)(2,1)S(1)}, bf16[16,4096]{1,0:T(8,128)(2,1)S(1)}, u32[]{:S(2)}, u32[]{:S(2)}) %collective-permute-start.13) | collective-permute-done | bytes 131104 | tf_op jit(solution)/shard_map/ppermute | solution.py:201
  262.8 0.9 fusion.8
  263.7 1.3 collective-permute-start.18
  265.0 5.7 %collective-permute-done.20.refs_7_ = bf16[16,4096]{1,0:T(8,128)(2,1)S(1)} collective-permute-done((bf16[16,4096]{1,0:T(8,128)(2,1)S(1)}, bf16[16,4096]{1,0:T(8,128)(2,1)S(1)}, u32[]{:S(2)}, u32[]{:S(2)}) %collective-permute-start.20) | collective-permute-done | bytes 131104 | tf_op jit(solution)/shard_map/ppermute | solution.py:192
  270.7 1.8 collective-permute-done.19.refs_6_
  273.1 1.9 collective-permute-done.17.refs_4_
  275.0 2.1 collective-permute-done.15.refs_2_
  277.1 1.5 collective-permute-done.14.refs_1_
  278.6 206.3 %peec_pairs.3 = (f32[16,4096]{1,0:T(8,128)S(1)}, bf16[16,4096]{1,0:T(8,128)(2,1)S(1)}, bf16[16,4096]{1,0:T(8,128)(2,1)S(1)}, bf16[16,4096]{1,0:T(8,128)(2,1)S(1)...) custom-call(s32[2,65]{1,0:T(2,128)S(1)} %broadcast_select_fusion.tab, ...), custom_call_target="tpu_custom_call" | custom-call | tf_op jit(solution)/shard_map/peec_pairs/pallas_call | solution.py:167
  484.9 2.3 collective-permute-start.21
  487.2 9.1 %collective-permute-start.22 = (bf16[16,4096]{1,0:T(8,128)(2,1)S(1)}, bf16[16,4096]{1,0:T(8,128)(2,1)S(1)}, u32[]{:S(2)}, u32[]{:S(2)}) collective-permute-start(bf16[16,4096]{1,0:T(8,128)(2,1)S(1)} %get-tuple-element.28), channel_id=1, source_target_pairs={{0,16},{1,17},{16,0},{17,1},{2,18},{3,19},{18,2},{19,3},{4,20},{5,... | collective-permute-start | bytes 393224 | tf_op jit(solution)/shard_map/ppermute | solution.py:201
  497.1 5.3 %collective-permute-done.22 = bf16[16,4096]{1,0:T(8,128)(2,1)S(1)} collective-permute-done((bf16[16,4096]{1,0:T(8,128)(2,1)S(1)}, bf16[16,4096]{1,0:T(8,128)(2,1)S(1)}, u32[]{:S(2)}, u32[]{:S(2)}) %collective-permute-start.22) | collective-permute-done | bytes 131104 | tf_op jit(solution)/shard_map/ppermute | solution.py:201
  502.5 1.7 collective-permute-done.23
  504.2 2.3 collective-permute-done.25
  506.5 3.1 collective-permute-done.26
  509.5 9.7 %collective-permute-done.27 = bf16[16,4096]{1,0:T(8,128)(2,1)S(1)} collective-permute-done((bf16[16,4096]{1,0:T(8,128)(2,1)S(1)}, bf16[16,4096]{1,0:T(8,128)(2,1)S(1)}, u32[]{:S(2)}, u32[]{:S(2)}) %collective-permute-start.27) | collective-permute-done | bytes 131104 | tf_op jit(solution)/shard_map/ppermute | solution.py:201
  519.2 0.8 convert_add_fusion
  (45 shorter events, 4.1 us)
Async XLA Ops:
  0.6 1.0 copy-start
  1.7 9.2 %collective-permute-start.6 = (bf16[16,4096]{1,0:T(8,128)(2,1)S(1)}, bf16[16,4096]{1,0:T(8,128)(2,1)S(1)}, u32[]{:S(2)}, u32[]{:S(2)}) collective-permute-start(bf16[16,4096]{1,0:T(8,128)(2,1)S(1)} %constant_dynamic-slice_fusion.refs_0_), channel_id=1, source_target_pairs={{19,0},{4,1},{7,16},{24,17},{21,2},{6,3},{9,18},{26,19},{23,4},{8,... | collective-permute-start | bytes 393224 | tf_op jit(solution)/shard_map/ppermute | solution.py:192
  4.2 16.0 %collective-permute-start.5 = (bf16[16,4096]{1,0:T(8,128)(2,1)S(1)}, bf16[16,4096]{1,0:T(8,128)(2,1)S(1)}, u32[]{:S(2)}, u32[]{:S(2)}) collective-permute-start(bf16[16,4096]{1,0:T(8,128)(2,1)S(1)} %constant_dynamic-slice_fusion.refs_0_), channel_id=1, source_target_pairs={{18,0},{21,1},{6,16},{9,17},{20,2},{23,3},{8,18},{11,19},{22,4},{2... | collective-permute-start | bytes 393224 | tf_op jit(solution)/shard_map/ppermute | solution.py:192
  4.4 16.9 %collective-permute-start.4 = (bf16[16,4096]{1,0:T(8,128)(2,1)S(1)}, bf16[16,4096]{1,0:T(8,128)(2,1)S(1)}, u32[]{:S(2)}, u32[]{:S(2)}) collective-permute-start(bf16[16,4096]{1,0:T(8,128)(2,1)S(1)} %constant_dynamic-slice_fusion.refs_0_), channel_id=1, source_target_pairs={{3,0},{20,1},{23,16},{8,17},{5,2},{22,3},{25,18},{10,19},{7,4},{24... | collective-permute-start | bytes 393224 | tf_op jit(solution)/shard_map/ppermute | solution.py:192
  6.8 14.4 %collective-permute-start.3 = (bf16[16,4096]{1,0:T(8,128)(2,1)S(1)}, bf16[16,4096]{1,0:T(8,128)(2,1)S(1)}, u32[]{:S(2)}, u32[]{:S(2)}) collective-permute-start(bf16[16,4096]{1,0:T(8,128)(2,1)S(1)} %constant_dynamic-slice_fusion.refs_0_), channel_id=1, source_target_pairs={{2,0},{5,1},{22,16},{25,17},{4,2},{7,3},{24,18},{27,19},{6,4},{9,5... | collective-permute-start | bytes 393224 | tf_op jit(solution)/shard_map/ppermute | solution.py:192
  7.7 13.6 %collective-permute-start.2 = (bf16[16,4096]{1,0:T(8,128)(2,1)S(1)}, bf16[16,4096]{1,0:T(8,128)(2,1)S(1)}, u32[]{:S(2)}, u32[]{:S(2)}) collective-permute-start(bf16[16,4096]{1,0:T(8,128)(2,1)S(1)} %constant_dynamic-slice_fusion.refs_0_), channel_id=1, source_target_pairs={{17,0},{0,1},{1,16},{16,17},{19,2},{2,3},{3,18},{18,19},{21,4},{4,... | collective-permute-start | bytes 393224 | tf_op jit(solution)/shard_map/ppermute | solution.py:190
  10.6 9.7 %copy-start.3 = (s32[2,65]{1,0:T(2,128)S(1)}, s32[2,65]{1,0:T(2,128)}, u32[]{:S(2)}) copy-start(s32[2,65]{1,0:T(2,128)} %constant.76.clone) | copy-start | bytes 1564
  10.9 9.4 %copy-start.2 = (s32[2,65]{1,0:T(2,128)S(1)}, s32[2,65]{1,0:T(2,128)}, u32[]{:S(2)}) copy-start(s32[2,65]{1,0:T(2,128)} %constant.77.clone) | copy-start | bytes 1564
  10.9 13.2 %collective-permute-start.1 = (bf16[16,4096]{1,0:T(8,128)(2,1)S(1)}, bf16[16,4096]{1,0:T(8,128)(2,1)S(1)}, u32[]{:S(2)}, u32[]{:S(2)}) collective-permute-start(bf16[16,4096]{1,0:T(8,128)(2,1)S(1)} %constant_dynamic-slice_fusion.refs_0_), channel_id=1, source_target_pairs={{16,0},{17,1},{0,16},{1,17},{18,2},{19,3},{2,18},{3,19},{20,4},{21... | collective-permute-start | bytes 393224 | tf_op jit(solution)/shard_map/ppermute | solution.py:190
  20.3 4.4 collective-permute-start
  21.2 241.6 %copy-start.1 = (f32[16,4096]{1,0:T(8,128)S(1)}, f32[16,4096]{1,0:T(8,128)}, u32[]{:S(2)}) copy-start(f32[16,4096]{1,0:T(8,128)} %param.6) | copy-start | bytes 786436
  230.7 11.1 %collective-permute-start.7 = (bf16[16,4096]{1,0:T(8,128)(2,1)S(1)}, bf16[16,4096]{1,0:T(8,128)(2,1)S(1)}, u32[]{:S(2)}, u32[]{:S(2)}) collective-permute-start(bf16[16,4096]{1,0:T(8,128)(2,1)S(1)} %get-tuple-element.19), channel_id=1, source_target_pairs={{0,1},{1,16},{16,17},{17,0},{2,3},{3,18},{18,19},{19,2},{4,5},{5,2... | collective-permute-start | bytes 393224 | tf_op jit(solution)/shard_map/ppermute | solution.py:201
  232.0 16.7 %collective-permute-start.8 = (bf16[16,4096]{1,0:T(8,128)(2,1)S(1)}, bf16[16,4096]{1,0:T(8,128)(2,1)S(1)}, u32[]{:S(2)}, u32[]{:S(2)}) collective-permute-start(bf16[16,4096]{1,0:T(8,128)(2,1)S(1)} %get-tuple-element.20), channel_id=1, source_target_pairs={{0,16},{1,17},{16,0},{17,1},{2,18},{3,19},{18,2},{19,3},{4,20},{5,... | collective-permute-start | bytes 393224 | tf_op jit(solution)/shard_map/ppermute | solution.py:201
  241.1 8.3 %collective-permute-start.9 = (bf16[16,4096]{1,0:T(8,128)(2,1)S(1)}, bf16[16,4096]{1,0:T(8,128)(2,1)S(1)}, u32[]{:S(2)}, u32[]{:S(2)}) collective-permute-start(bf16[16,4096]{1,0:T(8,128)(2,1)S(1)} %get-tuple-element.21), channel_id=1, source_target_pairs={{0,17},{1,0},{16,1},{17,16},{2,19},{3,2},{18,3},{19,18},{4,21},{5,... | collective-permute-start | bytes 393224 | tf_op jit(solution)/shard_map/ppermute | solution.py:201
  241.8 7.6 %collective-permute-start.10 = (bf16[16,4096]{1,0:T(8,128)(2,1)S(1)}, bf16[16,4096]{1,0:T(8,128)(2,1)S(1)}, u32[]{:S(2)}, u32[]{:S(2)}) collective-permute-start(bf16[16,4096]{1,0:T(8,128)(2,1)S(1)} %get-tuple-element.22), channel_id=1, source_target_pairs={{0,2},{1,5},{16,22},{17,25},{2,4},{3,7},{18,24},{19,27},{4,6},{5,9... | collective-permute-start | bytes 393224 | tf_op jit(solution)/shard_map/ppermute | solution.py:201
  241.8 9.4 %collective-permute-start.11 = (bf16[16,4096]{1,0:T(8,128)(2,1)S(1)}, bf16[16,4096]{1,0:T(8,128)(2,1)S(1)}, u32[]{:S(2)}, u32[]{:S(2)}) collective-permute-start(bf16[16,4096]{1,0:T(8,128)(2,1)S(1)} %get-tuple-element.23), channel_id=1, source_target_pairs={{0,3},{1,20},{16,23},{17,8},{2,5},{3,22},{18,25},{19,10},{4,7},{5,... | collective-permute-start | bytes 393224 | tf_op jit(solution)/shard_map/ppermute | solution.py:201
  241.8 11.6 %collective-permute-start.12 = (bf16[16,4096]{1,0:T(8,128)(2,1)S(1)}, bf16[16,4096]{1,0:T(8,128)(2,1)S(1)}, u32[]{:S(2)}, u32[]{:S(2)}) collective-permute-start(bf16[16,4096]{1,0:T(8,128)(2,1)S(1)} %get-tuple-element.24), channel_id=1, source_target_pairs={{0,18},{1,21},{16,6},{17,9},{2,20},{3,23},{18,8},{19,11},{4,22},{5... | collective-permute-start | bytes 393224 | tf_op jit(solution)/shard_map/ppermute | solution.py:201
  248.7 14.1 %collective-permute-start.13 = (bf16[16,4096]{1,0:T(8,128)(2,1)S(1)}, bf16[16,4096]{1,0:T(8,128)(2,1)S(1)}, u32[]{:S(2)}, u32[]{:S(2)}) collective-permute-start(bf16[16,4096]{1,0:T(8,128)(2,1)S(1)} %get-tuple-element.25), channel_id=1, source_target_pairs={{0,19},{1,4},{16,7},{17,24},{2,21},{3,6},{18,9},{19,26},{4,23},{5,... | collective-permute-start | bytes 393224 | tf_op jit(solution)/shard_map/ppermute | solution.py:201
  263.7 7.0 %collective-permute-start.20 = (bf16[16,4096]{1,0:T(8,128)(2,1)S(1)}, bf16[16,4096]{1,0:T(8,128)(2,1)S(1)}, u32[]{:S(2)}, u32[]{:S(2)}) collective-permute-start(bf16[16,4096]{1,0:T(8,128)(2,1)S(1)} %get-tuple-element.34.refs_0_), channel_id=1, source_target_pairs={{19,0},{4,1},{7,16},{24,17},{21,2},{6,3},{9,18},{26,19},{23,4},{8,... | collective-permute-start | bytes 393224 | tf_op jit(solution)/shard_map/ppermute | solution.py:192
  263.7 8.8 %collective-permute-start.19 = (bf16[16,4096]{1,0:T(8,128)(2,1)S(1)}, bf16[16,4096]{1,0:T(8,128)(2,1)S(1)}, u32[]{:S(2)}, u32[]{:S(2)}) collective-permute-start(bf16[16,4096]{1,0:T(8,128)(2,1)S(1)} %get-tuple-element.34.refs_0_), channel_id=1, source_target_pairs={{18,0},{21,1},{6,16},{9,17},{20,2},{23,3},{8,18},{11,19},{22,4},{2... | collective-permute-start | bytes 393224 | tf_op jit(solution)/shard_map/ppermute | solution.py:192
  263.7 9.4 %collective-permute-start.18 = (bf16[16,4096]{1,0:T(8,128)(2,1)S(1)}, bf16[16,4096]{1,0:T(8,128)(2,1)S(1)}, u32[]{:S(2)}, u32[]{:S(2)}) collective-permute-start(bf16[16,4096]{1,0:T(8,128)(2,1)S(1)} %get-tuple-element.34.refs_0_), channel_id=1, source_target_pairs={{3,0},{20,1},{23,16},{8,17},{5,2},{22,3},{25,18},{10,19},{7,4},{24... | collective-permute-start | bytes 393224 | tf_op jit(solution)/shard_map/ppermute | solution.py:192
  265.0 10.0 %collective-permute-start.17 = (bf16[16,4096]{1,0:T(8,128)(2,1)S(1)}, bf16[16,4096]{1,0:T(8,128)(2,1)S(1)}, u32[]{:S(2)}, u32[]{:S(2)}) collective-permute-start(bf16[16,4096]{1,0:T(8,128)(2,1)S(1)} %get-tuple-element.34.refs_0_), channel_id=1, source_target_pairs={{2,0},{5,1},{22,16},{25,17},{4,2},{7,3},{24,18},{27,19},{6,4},{9,5... | collective-permute-start | bytes 393224 | tf_op jit(solution)/shard_map/ppermute | solution.py:192
  265.0 10.0 %collective-permute-start.16 = (bf16[16,4096]{1,0:T(8,128)(2,1)S(1)}, bf16[16,4096]{1,0:T(8,128)(2,1)S(1)}, u32[]{:S(2)}, u32[]{:S(2)}) collective-permute-start(bf16[16,4096]{1,0:T(8,128)(2,1)S(1)} %get-tuple-element.34.refs_0_), channel_id=1, source_target_pairs={{17,0},{0,1},{1,16},{16,17},{19,2},{2,3},{3,18},{18,19},{21,4},{4,... | collective-permute-start | bytes 393224 | tf_op jit(solution)/shard_map/ppermute | solution.py:190
  270.7 6.4 %collective-permute-start.15 = (bf16[16,4096]{1,0:T(8,128)(2,1)S(1)}, bf16[16,4096]{1,0:T(8,128)(2,1)S(1)}, u32[]{:S(2)}, u32[]{:S(2)}) collective-permute-start(bf16[16,4096]{1,0:T(8,128)(2,1)S(1)} %get-tuple-element.34.refs_0_), channel_id=1, source_target_pairs={{16,0},{17,1},{0,16},{1,17},{18,2},{19,3},{2,18},{3,19},{20,4},{21... | collective-permute-start | bytes 393224 | tf_op jit(solution)/shard_map/ppermute | solution.py:190
  272.5 6.1 %collective-permute-start.14 = (bf16[16,4096]{1,0:T(8,128)(2,1)S(1)}, bf16[16,4096]{1,0:T(8,128)(2,1)S(1)}, u32[]{:S(2)}, u32[]{:S(2)}) collective-permute-start(bf16[16,4096]{1,0:T(8,128)(2,1)S(1)} %get-tuple-element.34.refs_0_), channel_id=1, source_target_pairs={{1,0},{16,1},{17,16},{0,17},{3,2},{18,3},{19,18},{2,19},{5,4},{20,... | collective-permute-start | bytes 393224 | tf_op jit(solution)/shard_map/ppermute | solution.py:190
  484.9 12.2 %collective-permute-start.21 = (bf16[16,4096]{1,0:T(8,128)(2,1)S(1)}, bf16[16,4096]{1,0:T(8,128)(2,1)S(1)}, u32[]{:S(2)}, u32[]{:S(2)}) collective-permute-start(bf16[16,4096]{1,0:T(8,128)(2,1)S(1)} %get-tuple-element.27), channel_id=1, source_target_pairs={{0,1},{1,16},{16,17},{17,0},{2,3},{3,18},{18,19},{19,2},{4,5},{5,2... | collective-permute-start | bytes 393224 | tf_op jit(solution)/shard_map/ppermute | solution.py:201
  487.2 15.3 %collective-permute-start.22 = (bf16[16,4096]{1,0:T(8,128)(2,1)S(1)}, bf16[16,4096]{1,0:T(8,128)(2,1)S(1)}, u32[]{:S(2)}, u32[]{:S(2)}) collective-permute-start(bf16[16,4096]{1,0:T(8,128)(2,1)S(1)} %get-tuple-element.28), channel_id=1, source_target_pairs={{0,16},{1,17},{16,0},{17,1},{2,18},{3,19},{18,2},{19,3},{4,20},{5,... | collective-permute-start | bytes 393224 | tf_op jit(solution)/shard_map/ppermute | solution.py:201
  496.3 7.9 %collective-permute-start.23 = (bf16[16,4096]{1,0:T(8,128)(2,1)S(1)}, bf16[16,4096]{1,0:T(8,128)(2,1)S(1)}, u32[]{:S(2)}, u32[]{:S(2)}) collective-permute-start(bf16[16,4096]{1,0:T(8,128)(2,1)S(1)} %get-tuple-element.29), channel_id=1, source_target_pairs={{0,17},{1,0},{16,1},{17,16},{2,19},{3,2},{18,3},{19,18},{4,21},{5,... | collective-permute-start | bytes 393224 | tf_op jit(solution)/shard_map/ppermute | solution.py:201
  497.1 7.1 %collective-permute-start.24 = (bf16[16,4096]{1,0:T(8,128)(2,1)S(1)}, bf16[16,4096]{1,0:T(8,128)(2,1)S(1)}, u32[]{:S(2)}, u32[]{:S(2)}) collective-permute-start(bf16[16,4096]{1,0:T(8,128)(2,1)S(1)} %get-tuple-element.30), channel_id=1, source_target_pairs={{0,2},{1,5},{16,22},{17,25},{2,4},{3,7},{18,24},{19,27},{4,6},{5,9... | collective-permute-start | bytes 393224 | tf_op jit(solution)/shard_map/ppermute | solution.py:201
  497.1 9.4 %collective-permute-start.25 = (bf16[16,4096]{1,0:T(8,128)(2,1)S(1)}, bf16[16,4096]{1,0:T(8,128)(2,1)S(1)}, u32[]{:S(2)}, u32[]{:S(2)}) collective-permute-start(bf16[16,4096]{1,0:T(8,128)(2,1)S(1)} %get-tuple-element.31), channel_id=1, source_target_pairs={{0,3},{1,20},{16,23},{17,8},{2,5},{3,22},{18,25},{19,10},{4,7},{5,... | collective-permute-start | bytes 393224 | tf_op jit(solution)/shard_map/ppermute | solution.py:201
  497.1 12.5 %collective-permute-start.26 = (bf16[16,4096]{1,0:T(8,128)(2,1)S(1)}, bf16[16,4096]{1,0:T(8,128)(2,1)S(1)}, u32[]{:S(2)}, u32[]{:S(2)}) collective-permute-start(bf16[16,4096]{1,0:T(8,128)(2,1)S(1)} %get-tuple-element.32), channel_id=1, source_target_pairs={{0,18},{1,21},{16,6},{17,9},{2,20},{3,23},{18,8},{19,11},{4,22},{5... | collective-permute-start | bytes 393224 | tf_op jit(solution)/shard_map/ppermute | solution.py:201
  502.5 16.7 %collective-permute-start.27 = (bf16[16,4096]{1,0:T(8,128)(2,1)S(1)}, bf16[16,4096]{1,0:T(8,128)(2,1)S(1)}, u32[]{:S(2)}, u32[]{:S(2)}) collective-permute-start(bf16[16,4096]{1,0:T(8,128)(2,1)S(1)} %get-tuple-element.33), channel_id=1, source_target_pairs={{0,19},{1,4},{16,7},{17,24},{2,21},{3,6},{18,9},{19,26},{4,23},{5,... | collective-permute-start | bytes 393224 | tf_op jit(solution)/shard_map/ppermute | solution.py:201
